TPU v7x, 32 devices: a whole 2x2x4 slice. The times are simulated.
32 devices in a mesh: row: 8 (over z, core), col: 4 (over y, x).
Axes of the slice: x: 2, y: 2, z: 4, core: 2. Of those that a mesh axis runs over, the one named last changes fastest.
Arguments:
- slab: float32 [16384, 1024], P('row', 'col'), may hold values from -6 to 6
- ranks: int32 [2, 1024], P(None, 'col'), may hold values from 0 to 1023, as said below
- poles: float32 [2, 1024], P(None, 'col'), as said below
- roots: float32 [2, 1024], P(None, 'col')
- flags: int32 [2, 1024], P(None, 'col'), may hold values 0 or 1
- reflectors: float32 [8, 16384], P(None, 'row'), may hold values from -0.5 to 0.5
- reflector_scales: float32 [8, 128], P(None, 'row'), may hold values from 1 to 1.6
Outputs:
- eigenvectors: float32 [16384, 1024], P('row', 'col')
Inputs may be any that keep to these rules, and one draw needn't show every extreme that they name: Within each aligned group of 512 entries of level one, and of 1024 entries of level two, the ranks are a permutation of the group's positions. At each level, every root differs from every pole of its group by 0.05 or more, and two poles of one group differ by 0.6 or more.
All inputs are finite; a program needn't handle non-finite values. No bound on the sum of `flags` on one device may be relied on, other than what follows from the above.
Results may differ from a plain program's by a relative error of at most 0.0003.
Values sent between devices are 32-bit elements; how exact they have to be, the bound alone decides.
A program may use at most 64 MiB of HBM per device.

v0:
```python
import functools

import jax
import jax.numpy as jnp
from jax import lax
from jax.experimental import pallas as pl
from jax.experimental.pallas import tpu as pltpu
from jax.sharding import PartitionSpec as P

BAND = 128
SETS = 8
ABOVE = 1024
BELOW = 128
CHUNK = 256
MESH = pl.DeviceIdType.MESH
F32 = jnp.float32
BF16 = jnp.bfloat16


def set_offset(index):
    return 1 + (SETS - 1 - index) * (BAND - 2) // (SETS - 1)


def halves(value):
    high = value.astype(BF16)
    low = (value - high.astype(F32)).astype(BF16)
    return high, low


def dot(left, right):
    return jnp.dot(left, right, preferred_element_type=F32)


def dot3(left, right_high, right_low):
    high, low = halves(left)
    return dot(high, right_high) + (dot(high, right_low) + dot(low, right_high))


def kernel(
    slab, ranks, poles, roots, flags, reflectors, scales, out,
    ext, refl, scales_own, scales_above, turned, gathered, tables, tall, wide,
    raw_ints, raw_floats, picked, shared, spread_weights,
    mix_one, mix_two, plan_high, plan_low, partial, arrived, result,
    local_sems, halo_send, halo_recv, table_send, table_recv,
    weight_send, weight_recv, gather_send, gather_recv, reduce_send, reduce_recv, out_sems,
):
    rows = slab.shape[0]
    width = slab.shape[1]
    chunks = rows // CHUNK
    windows = (rows + ABOVE) // BAND
    above_windows = ABOVE // BAND
    row = lax.axis_index("row")
    row_size = lax.axis_size("row")
    col = lax.axis_index("col")
    quarter = lax.rem(col, 4)
    quad = col - quarter
    near = quarter + 1 - 2 * lax.rem(quarter, 2)
    far = lax.rem(quarter + 2, 4)
    across = 3 - quarter
    near_id = (row, quad + near)
    far_id = (row, quad + far)
    across_id = (row, quad + across)
    has_prev = row > 0
    has_next = row < row_size - 1
    prev_id = (lax.max(row - 1, 0), col)
    next_id = (lax.min(row + 1, row_size - 1), col)

    own_rows = pl.ds(ABOVE, rows)
    own_slab = pltpu.make_async_copy(slab, ext.at[own_rows], local_sems.at[0])
    own_refl = pltpu.make_async_copy(reflectors, refl.at[:, own_rows], local_sems.at[1])
    own_scale_copy = pltpu.make_async_copy(scales, scales_own, local_sems.at[2])
    small = [
        pltpu.make_async_copy(ranks, raw_ints.at[0], local_sems.at[3]),
        pltpu.make_async_copy(flags, raw_ints.at[1], local_sems.at[4]),
        pltpu.make_async_copy(poles, raw_floats.at[0], local_sems.at[5]),
        pltpu.make_async_copy(roots, raw_floats.at[1], local_sems.at[6]),
    ]
    for copy in small:
        copy.start()
    own_refl.start()
    own_scale_copy.start()
    own_slab.start()

    barrier = pltpu.get_barrier_semaphore()
    for partner in (near_id, far_id, across_id):
        pl.semaphore_signal(barrier, inc=1, device_id=partner, device_id_type=MESH)

    @pl.when(has_prev)
    def _():
        pl.semaphore_signal(barrier, inc=1, device_id=prev_id, device_id_type=MESH)

    @pl.when(has_next)
    def _():
        pl.semaphore_signal(barrier, inc=1, device_id=next_id, device_id_type=MESH)

    for copy in small:
        copy.wait()
    tables[quarter] = jnp.concatenate(
        [raw_ints[0].astype(F32), raw_floats[0], raw_floats[1], raw_ints[1].astype(F32)], axis=0
    )

    pl.semaphore_wait(
        barrier, 3 + jnp.where(has_prev, 1, 0) + jnp.where(has_next, 1, 0)
    )

    def remote(source, target, send, recv, device):
        return pltpu.make_async_remote_copy(
            src_ref=source, dst_ref=target, send_sem=send, recv_sem=recv,
            device_id=device, device_id_type=MESH,
        )

    last = rows - ABOVE
    to_prev = [
        remote(reflectors.at[:, pl.ds(0, BELOW)], refl.at[:, pl.ds(ABOVE + rows, BELOW)],
               halo_send.at[0], halo_recv.at[0], prev_id),
        remote(slab.at[pl.ds(0, BELOW)], ext.at[pl.ds(ABOVE + rows, BELOW)],
               halo_send.at[1], halo_recv.at[1], prev_id),
    ]
    unread = set_offset(0) // 8 * 8
    to_next = [
        remote(slab.at[pl.ds(last + unread, ABOVE - unread)],
               ext.at[pl.ds(unread, ABOVE - unread)],
               halo_send.at[4], halo_recv.at[4], next_id),
        remote(reflectors.at[:, pl.ds(last, ABOVE)], refl.at[:, pl.ds(0, ABOVE)],
               halo_send.at[2], halo_recv.at[2], next_id),
        remote(scales, scales_above, halo_send.at[3], halo_recv.at[3], next_id),
    ]

    @pl.when(has_prev)
    def _():
        for copy in to_prev:
            copy.start()

    @pl.when(has_next)
    def _():
        for copy in to_next:
            copy.start()

    table_copies = [
        remote(tables.at[quarter], tables.at[quarter], table_send.at[i], table_recv.at[i], device)
        for i, device in enumerate((near_id, far_id, across_id))
    ]
    for copy in table_copies:
        copy.start()

    @pl.when(jnp.logical_not(has_prev))
    def _():
        ext[pl.ds(0, ABOVE)] = jnp.zeros((ABOVE, width), F32)
        refl[:, pl.ds(0, ABOVE)] = jnp.zeros((SETS, ABOVE), F32)
        scales_above[...] = jnp.zeros(scales_above.shape, F32)

    @pl.when(jnp.logical_not(has_next))
    def _():
        ext[pl.ds(ABOVE + rows, BELOW)] = jnp.zeros((BELOW, width), F32)
        refl[:, pl.ds(ABOVE + rows, BELOW)] = jnp.zeros((SETS, BELOW), F32)

    own_refl.wait()
    own_scale_copy.wait()
    own_slab.wait()

    @pl.when(has_next)
    def _():
        to_prev[0].wait_recv()
        to_prev[1].wait_recv()

    lane = lax.broadcasted_iota(jnp.int32, (SETS, BAND), 1)
    offsets = 1 + (SETS - 1 - lax.broadcasted_iota(jnp.int32, (SETS, BAND), 0)) * (
        (BAND - 2) // (SETS - 1)
    )

    def turn(block, low_scale, high_scale):
        spread = jnp.where(lane < offsets, low_scale, high_scale)
        both = jnp.concatenate([refl[:, block * BAND : (block + 1) * BAND], spread], axis=0)
        turned[block * BAND : (block + 1) * BAND, : 2 * SETS] = both.T

    own_scales = scales_own[...]

    def own_scale(window):
        index = min(max(window - above_windows, 0), own_scales.shape[1] - 1)
        return own_scales[:, index : index + 1]

    for block in range(above_windows, windows + 1):
        turn(block, own_scale(block - 1), own_scale(block))

    place = lax.broadcasted_iota(jnp.int32, (BAND + 8, 1), 0)

    def sweep(index, first, stop):
        offset = set_offset(index)
        base, shift = offset // 8 * 8, offset % 8
        inside = (place >= shift) & (place < BAND + shift)

        def window(w, carry):
            start = pl.multiple_of(w * BAND + base, 8)
            span = pl.ds(start, BAND + 8)
            blade = jnp.where(inside, turned[span, index : index + 1], 0.0)
            scale = turned[pl.ds(start + 8, 8), SETS + index : SETS + index + 1]
            panel = ext[span]
            projection = jnp.sum(blade * panel, axis=0, keepdims=True) * scale[:1]
            ext[span] = panel - blade * projection
            return carry

        lax.fori_loop(first, stop, window, 0, unroll=stop - first)

    def gather_copy(chunk, device):
        return remote(
            ext.at[pl.ds(ABOVE + chunk * CHUNK, CHUNK)],
            gathered.at[pl.ds(chunk * CHUNK, CHUNK)],
            gather_send.at[chunk], gather_recv.at[chunk], device,
        )

    def reduce_copy(chunk, device):
        span = pl.ds(chunk * CHUNK, CHUNK)
        return remote(
            partial.at[span], arrived.at[span],
            reduce_send.at[chunk], reduce_recv.at[chunk], device,
        )

    def send_chunk(chunk):
        gather_copy(chunk, near_id if chunk % 2 == 0 else far_id).start()

    half = ABOVE // CHUNK
    edge = above_windows + SETS
    for index in range(SETS):
        sweep(index, above_windows + index, edge + 2)
    send_chunk(half)
    first = edge + 2
    for chunk in range(half + 1, chunks):
        for index in range(SETS):
            sweep(index, first, first + CHUNK // BAND)
        first += CHUNK // BAND
        send_chunk(chunk)

    for copy in table_copies:
        copy.wait_recv()
    for i in range(4):
        wide[:, i * width : (i + 1) * width] = tables[i]
    for i in range(4 * width // BAND):
        tall[i * BAND : (i + 1) * BAND, :SETS] = wide[:, i * BAND : (i + 1) * BAND].T

    half_start = lax.rem(quarter // 2, 2) * 2 * width

    def pick(index, ranks_row, start, size):
        depth = 64
        positions = lax.broadcasted_iota(jnp.int32, (depth, 1), 0)

        def step(number, total):
            at = pl.ds(pl.multiple_of(start + number * depth, depth), depth)
            here = (positions + number * depth).astype(F32)
            root = tall[at, 4 + index : 5 + index]
            return total + jnp.sum(jnp.where(ranks_row == here, root, 0.0), axis=0, keepdims=True)

        return lax.fori_loop(0, size // depth, step, jnp.zeros((1, size), F32))

    group = quarter // 2
    half_ranks = jnp.concatenate(
        [tables[2 * group, 0:1], tables[2 * group + 1, 0:1]], axis=1
    )
    half_picked = pick(0, half_ranks, half_start, 2 * width)
    all_picked = pick(1, wide[1:2, :], 0, 4 * width)
    both = jnp.concatenate(
        [jnp.concatenate([half_picked, half_picked], axis=1), all_picked]
        + [jnp.zeros((6, 4 * width), F32)], axis=0
    )
    for i in range(4 * width // BAND):
        picked[i * BAND : (i + 1) * BAND, :SETS] = both[:, i * BAND : (i + 1) * BAND].T

    def weigh(index, start, size, own_start):
        depth = 64
        own = tables[quarter, 2 + index : 3 + index]
        own_place = own_start + lax.broadcasted_iota(jnp.int32, (1, width), 1)
        positions = lax.broadcasted_iota(jnp.int32, (depth, 1), 0)

        def step(number, total):
            at = pl.ds(pl.multiple_of(start + number * depth, depth), depth)
            within = pl.ds(pl.multiple_of(number * depth, depth), depth)
            pole = tall[at, 2 + index : 3 + index]
            living = tall[at, 6 + index : 7 + index] == 0.0
            root = picked[within, index : index + 1]
            between = jnp.where(positions + number * depth == own_place, 1.0, jnp.abs(pole - own))
            logs = jnp.log(jnp.abs(root - own) / between)
            return total + jnp.sum(jnp.where(living, logs, 0.0), axis=0, keepdims=True)

        total = lax.fori_loop(0, size // depth, step, jnp.zeros((1, width), F32), unroll=2)
        alive = tables[quarter, 6 + index : 7 + index] == 0.0
        return jnp.where(alive, jnp.exp(0.5 * total), 0.0)

    weight_one = weigh(0, half_start, 2 * width, lax.rem(quarter, 2) * width)
    weight_two = weigh(1, 0, 4 * width, quarter * width)
    shared[quarter] = jnp.concatenate([weight_one, weight_two, jnp.zeros((6, width), F32)], axis=0)
    weight_copies = [
        remote(shared.at[quarter], shared.at[quarter], weight_send.at[i], weight_recv.at[i], device)
        for i, device in enumerate((near_id, far_id, across_id))
    ]
    for copy in weight_copies:
        copy.start()

    def level(index, start, size, store, blocks):
        depth = 128

        def column(kind, step):
            at = pl.ds(pl.multiple_of(start + step * depth, depth), depth)
            return tall[at, 2 * kind + index : 2 * kind + index + 1]

        for number, (block, within) in enumerate(blocks):
            root_block = tables[block, 4 + index : 5 + index]
            here = (within * width + lax.broadcasted_iota(jnp.int32, (1, width), 1)).astype(F32)

            def cauchy(step, carry):
                norms, dead = carry
                at = pl.ds(pl.multiple_of(step * depth, depth), depth)
                shift = pl.ds(pl.multiple_of(start + step * depth, depth), depth)
                weight = spread_weights[shift, index : index + 1]
                value = weight / (column(1, step) - root_block)
                store[number, at] = value
                norms = norms + jnp.sum(value * value, axis=0, keepdims=True)
                match = column(0, step) == here
                dead = dead + jnp.sum(
                    jnp.where(match, column(3, step), 0.0), axis=0, keepdims=True
                )
                return norms, dead

            zero = jnp.zeros((1, width), F32)
            norms, dead = lax.fori_loop(0, size // depth, cauchy, (zero, zero), unroll=2)
            inverse = 1.0 / jnp.sqrt(norms)

            def finish(step, carry):
                at = pl.ds(pl.multiple_of(step * depth, depth), depth)
                match = (column(0, step) == here).astype(F32)
                store[number, at] = jnp.where(dead > 0.0, match, store[number, at] * inverse)
                return carry

            lax.fori_loop(0, size // depth, finish, 0, unroll=2)

    @pl.when(has_prev)
    def _():
        for copy in to_next:
            copy.wait_recv()

    halo_scales = jnp.where(has_prev, scales_above[...], 0.0)
    count = own_scales.shape[1]

    def any_scale(window):
        if window < 0:
            return jnp.zeros((SETS, 1), F32)
        if window < above_windows:
            index = count - above_windows + window
            return halo_scales[:, index : index + 1]
        return own_scale(window)

    for block in range(above_windows + 1):
        turn(block, any_scale(block - 1), any_scale(block))
    for index in range(SETS):
        sweep(index, index, above_windows + index)
    for chunk in range(half):
        send_chunk(chunk)

    for copy in weight_copies:
        copy.wait_recv()
    for i in range(4):
        for j in range(width // BAND):
            spread_weights[i * width + j * BAND : i * width + (j + 1) * BAND, :SETS] = shared[
                i, :, j * BAND : (j + 1) * BAND
            ].T
    for group in range(2):
        level(
            0, group * 2 * width, 2 * width, mix_one.at[group],
            [(2 * group, 0), (2 * group + 1, 1)],
        )
    level(1, 0, 4 * width, mix_two, [(quarter, quarter), (near, near), (far, far)])

    for which, (other, kept) in enumerate(((near, 2), (far, 1))):
        for part, source in enumerate((quarter, other)):
            group = source // 2
            at = pl.ds(pl.multiple_of(lax.rem(source, 2) * width, width), width)
            left = jnp.concatenate([mix_one[group, 0, at], mix_one[group, 1, at]], axis=1)
            under = pl.ds(pl.multiple_of(group * 2 * width, width), 2 * width)
            for side, block in enumerate((0, kept)):
                span = (which, slice(part * width, (part + 1) * width), slice(side * width, (side + 1) * width))
                if which == 1 and part == 0 and side == 0:
                    plan_high[span] = plan_high[(0,) + span[1:]]
                    plan_low[span] = plan_low[(0,) + span[1:]]
                    continue
                high, low = halves(mix_two[block, under])
                value = dot3(left, high, low)
                high, low = halves(value)
                plan_high[span] = high
                plan_low[span] = low

    def merge(step, carry):
        pair = lax.rem(step + half // 2, chunks // 2)
        for which in range(2):
            chunk = 2 * pair + which
            gather_copy(chunk, near_id if which == 0 else far_id).wait_recv()
            span = pl.ds(pl.multiple_of(chunk * CHUNK, CHUNK), CHUNK)
            mine = ext[pl.ds(pl.multiple_of(ABOVE + chunk * CHUNK, CHUNK), CHUNK)]
            left = jnp.concatenate([mine, gathered[span]], axis=1)
            away = slice(width, 2 * width)
            partial[span] = dot3(left, plan_high[which, :, away], plan_low[which, :, away])
            reduce_copy(chunk, far_id if which == 0 else near_id).start()
            home = slice(0, width)
            result[span] = dot3(left, plan_high[which, :, home], plan_low[which, :, home])
        return carry

    lax.fori_loop(0, chunks // 2, merge, 0)

    def out_copy(chunk):
        span = pl.ds(chunk * CHUNK, CHUNK)
        return pltpu.make_async_copy(result.at[span], out.at[span], out_sems.at[chunk])

    def collect(step, carry):
        pair = lax.rem(step + half // 2, chunks // 2)
        for which in range(2):
            chunk = 2 * pair + which
            reduce_copy(chunk, far_id if which == 0 else near_id).wait_recv()
            span = pl.ds(pl.multiple_of(chunk * CHUNK, CHUNK), CHUNK)
            result[span] = result[span] + arrived[span]
            out_copy(chunk).start()
        return carry

    lax.fori_loop(0, chunks // 2, collect, 0)

    for chunk in range(chunks):
        gather_copy(chunk, near_id if chunk % 2 == 0 else far_id).wait_send()
        reduce_copy(chunk, far_id if chunk % 2 == 0 else near_id).wait_send()
        out_copy(chunk).wait()
    for copy in table_copies + weight_copies:
        copy.wait_send()

    @pl.when(has_prev)
    def _():
        for copy in to_prev:
            copy.wait_send()

    @pl.when(has_next)
    def _():
        for copy in to_next:
            copy.wait_send()


def per_device(slab, ranks, poles, roots, flags, reflectors, reflector_scales):
    rows, width = slab.shape
    chunks = rows // CHUNK
    total = ABOVE + rows + BELOW
    anywhere = pl.BlockSpec(memory_space=pl.ANY)
    dma = pltpu.SemaphoreType.DMA
    return pl.pallas_call(
        kernel,
        out_shape=jax.ShapeDtypeStruct((rows, width), F32),
        in_specs=[anywhere] * 7,
        out_specs=anywhere,
        scratch_shapes=[
            pltpu.VMEM((total, width), F32),
            pltpu.VMEM((SETS, total), F32),
            pltpu.VMEM(reflector_scales.shape, F32),
            pltpu.VMEM(reflector_scales.shape, F32),
            pltpu.VMEM((total, 128), F32),
            pltpu.VMEM((rows, width), F32),
            pltpu.VMEM((4, 8, width), F32),
            pltpu.VMEM((4 * width, 128), F32),
            pltpu.VMEM((8, 4 * width), F32),
            pltpu.VMEM((2, 2, width), jnp.int32),
            pltpu.VMEM((2, 2, width), F32),
            pltpu.VMEM((4 * width, 128), F32),
            pltpu.VMEM((4, 8, width), F32),
            pltpu.VMEM((4 * width, 128), F32),
            pltpu.VMEM((2, 2, 2 * width, width), F32),
            pltpu.VMEM((3, 4 * width, width), F32),
            pltpu.VMEM((2, 2 * width, 2 * width), BF16),
            pltpu.VMEM((2, 2 * width, 2 * width), BF16),
            pltpu.VMEM((rows, width), F32),
            pltpu.VMEM((rows, width), F32),
            pltpu.VMEM((rows, width), F32),
            dma((7,)), dma((5,)), dma((5,)), dma((3,)), dma((3,)), dma((3,)), dma((3,)),
            dma((chunks,)), dma((chunks,)), dma((chunks,)), dma((chunks,)), dma((chunks,)),
        ],
        compiler_params=pltpu.CompilerParams(
            collective_id=0, has_side_effects=True, vmem_limit_bytes=48 * 1024 * 1024
        ),
    )(slab, ranks, poles, roots, flags, reflectors, reflector_scales)


def solution(mesh):
    return jax.shard_map(
        per_device,
        mesh=mesh,
        in_specs=(
            P("row", "col"),
            P(None, "col"),
            P(None, "col"),
            P(None, "col"),
            P(None, "col"),
            P(None, "row"),
            P(None, "row"),
        ),
        out_specs=P("row", "col"),
        check_vma=False,
    )
```

profile of v0, /device:TPU:1, one launch (start us, length us, event | category | flops | bytes accessed | tf_op | source)
XLA Modules:
  0.0 62.6 jit_solution(15720484151389577181)
XLA Ops:
  0.0 0.0 copy-start
  0.0 1.6 %copy-done = f32[2048,256]{1,0:T(8,128)S(1)} copy-done((f32[2048,256]{1,0:T(8,128)S(1)}, f32[2048,256]{1,0:T(8,128)}, u32[]{:S(2)}) %copy-start) | copy-done | bytes 2097176
  1.6 0.0 copy-start.1
  1.6 0.8 %copy-done.1 = f32[8,2048]{1,0:T(8,128)S(1)} copy-done((f32[8,2048]{1,0:T(8,128)S(1)}, f32[8,2048]{1,0:T(8,128)}, u32[]{:S(2)}) %copy-start.1) | copy-done | bytes 65560
  2.4 0.0 copy-start.2
  2.4 0.7 %copy-done.2 = f32[8,16]{1,0:T(8,128)S(1)} copy-done((f32[8,16]{1,0:T(8,128)S(1)}, f32[8,16]{1,0:T(8,128)}, u32[]{:S(2)}) %copy-start.2) | copy-done | bytes 536
  3.1 0.0 copy-start.3
  3.1 0.7 %copy-done.3 = s32[2,256]{1,0:T(2,128)S(1)} copy-done((s32[2,256]{1,0:T(2,128)S(1)}, s32[2,256]{1,0:T(2,128)}, u32[]{:S(2)}) %copy-start.3) | copy-done | bytes 2072
  3.8 0.0 copy-start.4
  3.8 0.7 %copy-done.4 = f32[2,256]{1,0:T(2,128)S(1)} copy-done((f32[2,256]{1,0:T(2,128)S(1)}, f32[2,256]{1,0:T(2,128)}, u32[]{:S(2)}) %copy-start.4) | copy-done | bytes 2072
  4.5 0.0 copy-start.5
  4.5 0.7 %copy-done.5 = f32[2,256]{1,0:T(2,128)S(1)} copy-done((f32[2,256]{1,0:T(2,128)S(1)}, f32[2,256]{1,0:T(2,128)}, u32[]{:S(2)}) %copy-start.5) | copy-done | bytes 2072
  5.2 0.0 copy-start.6
  5.2 0.7 %copy-done.6 = s32[2,256]{1,0:T(2,128)S(1)} copy-done((s32[2,256]{1,0:T(2,128)S(1)}, s32[2,256]{1,0:T(2,128)}, u32[]{:S(2)}) %copy-start.6) | copy-done | bytes 2072
  5.8 55.5 %shard_map.73 = f32[2048,256]{1,0:T(8,128)S(1)} custom-call(f32[2048,256]{1,0:T(8,128)S(1)} %copy-done, s32[2,256]{1,0:T(2,128)S(1)} %copy-done.3, f32[2,256]{1,0:T(2,128)S(1)} %copy-done.4, f32[2,256]{1,0:T(2,128)S(1)} %copy-done.5, s32[2,256]{1,0:T(2,128)S(1)} %copy-done.6, f32[8,2048]{1,0:T(8,128)S(1)} %copy-done.1, f32[8,16]{1,0:T(8,128)S(1)} %copy-done.2), custom_call_target="tpu_custom_call" | custom-call | tf_op jit(solution)/shard_map/pallas_call | solution.py:446
  61.3 1.3 %copy.9 = f32[2048,256]{1,0:T(8,128)} copy(f32[2048,256]{1,0:T(8,128)S(1)} %shard_map.73) | data formatting | bytes 4194304
Async XLA Ops:
  0.0 1.6 %copy-start = (f32[2048,256]{1,0:T(8,128)S(1)}, f32[2048,256]{1,0:T(8,128)}, u32[]{:S(2)}) copy-start(f32[2048,256]{1,0:T(8,128)} %slab.1) | copy-start | bytes 6291460
  1.6 0.8 %copy-start.1 = (f32[8,2048]{1,0:T(8,128)S(1)}, f32[8,2048]{1,0:T(8,128)}, u32[]{:S(2)}) copy-start(f32[8,2048]{1,0:T(8,128)} %reflectors.1) | copy-start | bytes 196612
  2.4 0.7 %copy-start.2 = (f32[8,16]{1,0:T(8,128)S(1)}, f32[8,16]{1,0:T(8,128)}, u32[]{:S(2)}) copy-start(f32[8,16]{1,0:T(8,128)} %scales.1) | copy-start | bytes 1540
  3.1 0.7 %copy-start.3 = (s32[2,256]{1,0:T(2,128)S(1)}, s32[2,256]{1,0:T(2,128)}, u32[]{:S(2)}) copy-start(s32[2,256]{1,0:T(2,128)} %ranks.1) | copy-start | bytes 6148
  3.8 0.7 %copy-start.4 = (f32[2,256]{1,0:T(2,128)S(1)}, f32[2,256]{1,0:T(2,128)}, u32[]{:S(2)}) copy-start(f32[2,256]{1,0:T(2,128)} %poles.1) | copy-start | bytes 6148
  4.5 0.7 %copy-start.5 = (f32[2,256]{1,0:T(2,128)S(1)}, f32[2,256]{1,0:T(2,128)}, u32[]{:S(2)}) copy-start(f32[2,256]{1,0:T(2,128)} %roots.1) | copy-start | bytes 6148
  5.2 0.7 %copy-start.6 = (s32[2,256]{1,0:T(2,128)S(1)}, s32[2,256]{1,0:T(2,128)}, u32[]{:S(2)}) copy-start(s32[2,256]{1,0:T(2,128)} %flags.1) | copy-start | bytes 6148
where the time goes:
time: 62.9 us; the launch traced here: 62.6 us
  Pallas kernels  55.5 us (88%)
  local copies, waits for them, and re-layouts  7.16 us (11%)
    pallas_call x1, Pallas kernels, per_device(): pl.pallas_call(kernel, out_shape=jax.ShapeDtypeStruct((rows, width), F32)...  55.5 us
    unnamed x15, local copies, waits for them, and re-layouts  7.16 us

commit v1 on v0

--- a/solution.py
+++ b/solution.py
@@ -40,9 +40,9 @@
     slab, ranks, poles, roots, flags, reflectors, scales, out,
     ext, refl, scales_own, scales_above, turned, gathered, tables, tall, wide,
     raw_ints, raw_floats, picked, shared, spread_weights,
-    mix_one, mix_two, plan_high, plan_low, partial, arrived, result,
+    mix_one, mix_two, plan_high, plan_low, partial, arrived,
     local_sems, halo_send, halo_recv, table_send, table_recv,
-    weight_send, weight_recv, gather_send, gather_recv, reduce_send, reduce_recv, out_sems,
+    weight_send, weight_recv, gather_send, gather_recv, reduce_send, reduce_recv,
 ):
     rows = slab.shape[0]
     width = slab.shape[1]
@@ -398,14 +398,10 @@
             partial[span] = dot3(left, plan_high[which, :, away], plan_low[which, :, away])
             reduce_copy(chunk, far_id if which == 0 else near_id).start()
             home = slice(0, width)
-            result[span] = dot3(left, plan_high[which, :, home], plan_low[which, :, home])
+            out[span] = dot3(left, plan_high[which, :, home], plan_low[which, :, home])
         return carry
 
     lax.fori_loop(0, chunks // 2, merge, 0)
-
-    def out_copy(chunk):
-        span = pl.ds(chunk * CHUNK, CHUNK)
-        return pltpu.make_async_copy(result.at[span], out.at[span], out_sems.at[chunk])
 
     def collect(step, carry):
         pair = lax.rem(step + half // 2, chunks // 2)
@@ -413,8 +409,7 @@
             chunk = 2 * pair + which
             reduce_copy(chunk, far_id if which == 0 else near_id).wait_recv()
             span = pl.ds(pl.multiple_of(chunk * CHUNK, CHUNK), CHUNK)
-            result[span] = result[span] + arrived[span]
-            out_copy(chunk).start()
+            out[span] = out[span] + arrived[span]
         return carry
 
     lax.fori_loop(0, chunks // 2, collect, 0)
@@ -422,7 +417,6 @@
     for chunk in range(chunks):
         gather_copy(chunk, near_id if chunk % 2 == 0 else far_id).wait_send()
         reduce_copy(chunk, far_id if chunk % 2 == 0 else near_id).wait_send()
-        out_copy(chunk).wait()
     for copy in table_copies + weight_copies:
         copy.wait_send()
 
@@ -443,11 +437,13 @@
     total = ABOVE + rows + BELOW
     anywhere = pl.BlockSpec(memory_space=pl.ANY)
     dma = pltpu.SemaphoreType.DMA
+    operands = (slab, ranks, poles, roots, flags, reflectors, reflector_scales)
+    held = [pltpu.with_memory_space_constraint(x, pltpu.HBM) for x in operands]
     return pl.pallas_call(
         kernel,
-        out_shape=jax.ShapeDtypeStruct((rows, width), F32),
+        out_shape=pltpu.VMEM((rows, width), F32),
         in_specs=[anywhere] * 7,
-        out_specs=anywhere,
+        out_specs=pl.BlockSpec(memory_space=pltpu.VMEM),
         scratch_shapes=[
             pltpu.VMEM((total, width), F32),
             pltpu.VMEM((SETS, total), F32),
@@ -469,14 +465,13 @@
             pltpu.VMEM((2, 2 * width, 2 * width), BF16),
             pltpu.VMEM((rows, width), F32),
             pltpu.VMEM((rows, width), F32),
-            pltpu.VMEM((rows, width), F32),
             dma((7,)), dma((5,)), dma((5,)), dma((3,)), dma((3,)), dma((3,)), dma((3,)),
-            dma((chunks,)), dma((chunks,)), dma((chunks,)), dma((chunks,)), dma((chunks,)),
+            dma((chunks,)), dma((chunks,)), dma((chunks,)), dma((chunks,)),
         ],
         compiler_params=pltpu.CompilerParams(
             collective_id=0, has_side_effects=True, vmem_limit_bytes=48 * 1024 * 1024
         ),
-    )(slab, ranks, poles, roots, flags, reflectors, reflector_scales)
+    )(*held)
 
 
 def solution(mesh):

time: 62.9 us -> 56.7 us (0.901)
  local copies, waits for them, and re-layouts: 7.16 us -> 1.32 us
    unnamed x15 -> x1, local copies, waits for them, and re-layouts: 7.16 us -> 1.32 us
where the time goes in v1:
time: 56.7 us; the launch traced here: 56.5 us
  Pallas kernels  55.2 us (97%)
  local copies, waits for them, and re-layouts  1.32 us (2%)
    pallas_call x1, Pallas kernels, per_device(): pl.pallas_call(kernel, out_shape=pltpu.VMEM((rows, width), F32), in_specs...  55.2 us
    unnamed x1, local copies, waits for them, and re-layouts  1.32 us

profile of v1, /device:TPU:1, one launch (start us, length us, event | category | flops | bytes accessed | tf_op | source)
XLA Modules:
  0.0 56.5 jit_solution(16586930713352142706)
XLA Ops:
  0.0 55.2 %shard_map.73 = f32[2048,256]{1,0:T(8,128)S(1)} custom-call(f32[2048,256]{1,0:T(8,128)} %slab.1, s32[2,256]{1,0:T(2,128)} %ranks.1, f32[2,256]{1,0:T(2,128)} %poles.1, f32[2,256]{1,0:T(2,128)} %roots.1, s32[2,256]{1,0:T(2,128)} %flags.1, f32[8,2048]{1,0:T(8,128)} %reflectors.1, f32[8,16]{1,0:T(8,128)} %scales.1), custom_call_target="tpu_custom_call" | custom-call | tf_op jit(solution)/shard_map/pallas_call | solution.py:442
  55.2 1.3 %copy.9 = f32[2048,256]{1,0:T(8,128)} copy(f32[2048,256]{1,0:T(8,128)S(1)} %shard_map.73) | data formatting | bytes 4194304

commit v2 on v1

--- a/solution.py
+++ b/solution.py
@@ -9,9 +9,9 @@
 
 BAND = 128
 SETS = 8
-ABOVE = 1024
 BELOW = 128
 CHUNK = 256
+RAW = 2
 MESH = pl.DeviceIdType.MESH
 F32 = jnp.float32
 BF16 = jnp.bfloat16
@@ -38,17 +38,16 @@
 
 def kernel(
     slab, ranks, poles, roots, flags, reflectors, scales, out,
-    ext, refl, scales_own, scales_above, turned, gathered, tables, tall, wide,
-    raw_ints, raw_floats, picked, shared, spread_weights,
+    ext, refl, scales_own, turned, gathered, tables, tall, wide,
+    raw_ints, raw_floats, picked, shared, spread_weights, projections, above, fixes,
     mix_one, mix_two, plan_high, plan_low, partial, arrived,
-    local_sems, halo_send, halo_recv, table_send, table_recv,
+    local_sems, halo_send, halo_recv, table_send, table_recv, fix_send, fix_recv,
     weight_send, weight_recv, gather_send, gather_recv, reduce_send, reduce_recv,
 ):
     rows = slab.shape[0]
     width = slab.shape[1]
     chunks = rows // CHUNK
-    windows = (rows + ABOVE) // BAND
-    above_windows = ABOVE // BAND
+    windows = rows // BAND
     row = lax.axis_index("row")
     row_size = lax.axis_size("row")
     col = lax.axis_index("col")
@@ -65,7 +64,7 @@
     prev_id = (lax.max(row - 1, 0), col)
     next_id = (lax.min(row + 1, row_size - 1), col)
 
-    own_rows = pl.ds(ABOVE, rows)
+    own_rows = pl.ds(0, rows)
     own_slab = pltpu.make_async_copy(slab, ext.at[own_rows], local_sems.at[0])
     own_refl = pltpu.make_async_copy(reflectors, refl.at[:, own_rows], local_sems.at[1])
     own_scale_copy = pltpu.make_async_copy(scales, scales_own, local_sems.at[2])
@@ -109,32 +108,17 @@
             device_id=device, device_id_type=MESH,
         )
 
-    last = rows - ABOVE
     to_prev = [
-        remote(reflectors.at[:, pl.ds(0, BELOW)], refl.at[:, pl.ds(ABOVE + rows, BELOW)],
+        remote(reflectors.at[:, pl.ds(0, BELOW)], refl.at[:, pl.ds(rows, BELOW)],
                halo_send.at[0], halo_recv.at[0], prev_id),
-        remote(slab.at[pl.ds(0, BELOW)], ext.at[pl.ds(ABOVE + rows, BELOW)],
+        remote(slab.at[pl.ds(0, BELOW)], ext.at[pl.ds(rows, BELOW)],
                halo_send.at[1], halo_recv.at[1], prev_id),
     ]
-    unread = set_offset(0) // 8 * 8
-    to_next = [
-        remote(slab.at[pl.ds(last + unread, ABOVE - unread)],
-               ext.at[pl.ds(unread, ABOVE - unread)],
-               halo_send.at[4], halo_recv.at[4], next_id),
-        remote(reflectors.at[:, pl.ds(last, ABOVE)], refl.at[:, pl.ds(0, ABOVE)],
-               halo_send.at[2], halo_recv.at[2], next_id),
-        remote(scales, scales_above, halo_send.at[3], halo_recv.at[3], next_id),
-    ]
-
-    @pl.when(has_prev)
-    def _():
-        for copy in to_prev:
-            copy.start()
-
-    @pl.when(has_next)
-    def _():
-        for copy in to_next:
-            copy.start()
+    per_chunk = CHUNK // BAND
+    kept_first = (chunks - RAW) * per_chunk - 1
+    last_window = (windows - 1 - kept_first) * SETS
+    to_next = remote(projections.at[pl.ds(last_window, SETS)], above,
+                     halo_send.at[2], halo_recv.at[2], next_id)
 
     table_copies = [
         remote(tables.at[quarter], tables.at[quarter], table_send.at[i], table_recv.at[i], device)
@@ -143,67 +127,10 @@
     for copy in table_copies:
         copy.start()
 
-    @pl.when(jnp.logical_not(has_prev))
-    def _():
-        ext[pl.ds(0, ABOVE)] = jnp.zeros((ABOVE, width), F32)
-        refl[:, pl.ds(0, ABOVE)] = jnp.zeros((SETS, ABOVE), F32)
-        scales_above[...] = jnp.zeros(scales_above.shape, F32)
-
-    @pl.when(jnp.logical_not(has_next))
-    def _():
-        ext[pl.ds(ABOVE + rows, BELOW)] = jnp.zeros((BELOW, width), F32)
-        refl[:, pl.ds(ABOVE + rows, BELOW)] = jnp.zeros((SETS, BELOW), F32)
-
-    own_refl.wait()
-    own_scale_copy.wait()
-    own_slab.wait()
-
-    @pl.when(has_next)
-    def _():
-        to_prev[0].wait_recv()
-        to_prev[1].wait_recv()
-
-    lane = lax.broadcasted_iota(jnp.int32, (SETS, BAND), 1)
-    offsets = 1 + (SETS - 1 - lax.broadcasted_iota(jnp.int32, (SETS, BAND), 0)) * (
-        (BAND - 2) // (SETS - 1)
-    )
-
-    def turn(block, low_scale, high_scale):
-        spread = jnp.where(lane < offsets, low_scale, high_scale)
-        both = jnp.concatenate([refl[:, block * BAND : (block + 1) * BAND], spread], axis=0)
-        turned[block * BAND : (block + 1) * BAND, : 2 * SETS] = both.T
-
-    own_scales = scales_own[...]
-
-    def own_scale(window):
-        index = min(max(window - above_windows, 0), own_scales.shape[1] - 1)
-        return own_scales[:, index : index + 1]
-
-    for block in range(above_windows, windows + 1):
-        turn(block, own_scale(block - 1), own_scale(block))
-
-    place = lax.broadcasted_iota(jnp.int32, (BAND + 8, 1), 0)
-
-    def sweep(index, first, stop):
-        offset = set_offset(index)
-        base, shift = offset // 8 * 8, offset % 8
-        inside = (place >= shift) & (place < BAND + shift)
-
-        def window(w, carry):
-            start = pl.multiple_of(w * BAND + base, 8)
-            span = pl.ds(start, BAND + 8)
-            blade = jnp.where(inside, turned[span, index : index + 1], 0.0)
-            scale = turned[pl.ds(start + 8, 8), SETS + index : SETS + index + 1]
-            panel = ext[span]
-            projection = jnp.sum(blade * panel, axis=0, keepdims=True) * scale[:1]
-            ext[span] = panel - blade * projection
-            return carry
-
-        lax.fori_loop(first, stop, window, 0, unroll=stop - first)
-
     def gather_copy(chunk, device):
+        held = slab if isinstance(chunk, int) and chunk >= chunks - RAW else ext
         return remote(
-            ext.at[pl.ds(ABOVE + chunk * CHUNK, CHUNK)],
+            held.at[pl.ds(chunk * CHUNK, CHUNK)],
             gathered.at[pl.ds(chunk * CHUNK, CHUNK)],
             gather_send.at[chunk], gather_recv.at[chunk], device,
         )
@@ -218,17 +145,54 @@
     def send_chunk(chunk):
         gather_copy(chunk, near_id if chunk % 2 == 0 else far_id).start()
 
-    half = ABOVE // CHUNK
-    edge = above_windows + SETS
+    for chunk in range(chunks - RAW, chunks):
+        send_chunk(chunk)
+
+    @pl.when(has_prev)
+    def _():
+        for copy in to_prev:
+            copy.start()
+
+    @pl.when(jnp.logical_not(has_prev))
+    def _():
+        above[...] = jnp.zeros((SETS, width), F32)
+
+    @pl.when(jnp.logical_not(has_next))
+    def _():
+        ext[pl.ds(rows, BELOW)] = jnp.zeros((BELOW, width), F32)
+        refl[:, pl.ds(rows, BELOW)] = jnp.zeros((SETS, BELOW), F32)
+
+    own_refl.wait()
+    own_scale_copy.wait()
+
+    def turn(block):
+        span = slice(block * BAND, (block + 1) * BAND)
+        turned[span, :SETS] = refl[:, span].T
+
+    for block in range(windows):
+        turn(block)
+
+    place = lax.broadcasted_iota(jnp.int32, (BAND + 8, 1), 0)
+    own_scales = scales_own[...]
+
+    def sweep(index, number):
+        offset = set_offset(index)
+        base, shift = offset // 8 * 8, offset % 8
+        inside = (place >= shift) & (place < BAND + shift)
+        span = slice(number * BAND + base, number * BAND + base + BAND + 8)
+        blade = jnp.where(inside, turned[span, index : index + 1], 0.0)
+        panel = ext[span]
+        projection = jnp.sum(blade * panel, axis=0, keepdims=True)
+        projection = projection * own_scales[index : index + 1, number : number + 1]
+        if number >= kept_first:
+            at = (number - kept_first) * SETS + index
+            projections[at : at + 1] = projection
+        ext[span] = panel - blade * projection
+
+    own_slab.wait()
     for index in range(SETS):
-        sweep(index, above_windows + index, edge + 2)
-    send_chunk(half)
-    first = edge + 2
-    for chunk in range(half + 1, chunks):
-        for index in range(SETS):
-            sweep(index, first, first + CHUNK // BAND)
-        first += CHUNK // BAND
-        send_chunk(chunk)
+        for number in range(index, windows - 1):
+            sweep(index, number)
 
     for copy in table_copies:
         copy.wait_recv()
@@ -239,6 +203,9 @@
 
     half_start = lax.rem(quarter // 2, 2) * 2 * width
 
+    def fold(value):
+        return jnp.sum(value.reshape(value.shape[0] // 8, 8, value.shape[1]), axis=0)
+
     def pick(index, ranks_row, start, size):
         depth = 64
         positions = lax.broadcasted_iota(jnp.int32, (depth, 1), 0)
@@ -247,9 +214,10 @@
             at = pl.ds(pl.multiple_of(start + number * depth, depth), depth)
             here = (positions + number * depth).astype(F32)
             root = tall[at, 4 + index : 5 + index]
-            return total + jnp.sum(jnp.where(ranks_row == here, root, 0.0), axis=0, keepdims=True)
-
-        return lax.fori_loop(0, size // depth, step, jnp.zeros((1, size), F32))
+            return total + fold(jnp.where(ranks_row == here, root, 0.0))
+
+        total = lax.fori_loop(0, size // depth, step, jnp.zeros((8, size), F32))
+        return jnp.sum(total, axis=0, keepdims=True)
 
     group = quarter // 2
     half_ranks = jnp.concatenate(
@@ -278,11 +246,25 @@
             root = picked[within, index : index + 1]
             between = jnp.where(positions + number * depth == own_place, 1.0, jnp.abs(pole - own))
             logs = jnp.log(jnp.abs(root - own) / between)
-            return total + jnp.sum(jnp.where(living, logs, 0.0), axis=0, keepdims=True)
-
-        total = lax.fori_loop(0, size // depth, step, jnp.zeros((1, width), F32), unroll=2)
+            return total + fold(jnp.where(living, logs, 0.0))
+
+        total = lax.fori_loop(0, size // depth, step, jnp.zeros((8, width), F32), unroll=2)
+        total = jnp.sum(total, axis=0, keepdims=True)
         alive = tables[quarter, 6 + index : 7 + index] == 0.0
         return jnp.where(alive, jnp.exp(0.5 * total), 0.0)
+
+    @pl.when(has_next)
+    def _():
+        for copy in to_prev:
+            copy.wait_recv()
+
+    turn(windows)
+    for index in range(SETS):
+        sweep(index, windows - 1)
+
+    @pl.when(has_next)
+    def _():
+        to_next.start()
 
     weight_one = weigh(0, half_start, 2 * width, lax.rem(quarter, 2) * width)
     weight_two = weigh(1, 0, 4 * width, quarter * width)
@@ -293,6 +275,8 @@
     ]
     for copy in weight_copies:
         copy.start()
+    for chunk in range(chunks - 2 * RAW, chunks - RAW):
+        send_chunk(chunk)
 
     def level(index, start, size, store, blocks):
         depth = 128
@@ -331,28 +315,28 @@
 
             lax.fori_loop(0, size // depth, finish, 0, unroll=2)
 
+    fix_rows = (RAW // 2 * per_chunk + 2) * SETS
+    fix_copies = [
+        remote(projections.at[pl.ds(i * SETS, fix_rows)], fixes.at[i],
+               fix_send.at[i], fix_recv.at[i], device)
+        for i, device in enumerate((near_id, far_id))
+    ]
+    for copy in fix_copies:
+        copy.start()
+
     @pl.when(has_prev)
     def _():
-        for copy in to_next:
-            copy.wait_recv()
-
-    halo_scales = jnp.where(has_prev, scales_above[...], 0.0)
-    count = own_scales.shape[1]
-
-    def any_scale(window):
-        if window < 0:
-            return jnp.zeros((SETS, 1), F32)
-        if window < above_windows:
-            index = count - above_windows + window
-            return halo_scales[:, index : index + 1]
-        return own_scale(window)
-
-    for block in range(above_windows + 1):
-        turn(block, any_scale(block - 1), any_scale(block))
+        to_next.wait_recv()
+
+    head = lax.broadcasted_iota(jnp.int32, (BAND, 1), 0)
     for index in range(SETS):
-        sweep(index, index, above_windows + index)
-    for chunk in range(half):
-        send_chunk(chunk)
+        blade = jnp.where(head < set_offset(index), turned[:BAND, index : index + 1], 0.0)
+        ext[:BAND] = ext[:BAND] - blade * above[index : index + 1]
+        for number in range(index):
+            sweep(index, number)
+    for pair in reversed(range(chunks // 2 - RAW)):
+        send_chunk(2 * pair)
+        send_chunk(2 * pair + 1)
 
     for copy in weight_copies:
         copy.wait_recv()
@@ -386,13 +370,34 @@
                 plan_high[span] = high
                 plan_low[span] = low
 
+    for which, chunk in enumerate(range(chunks - RAW, chunks)):
+        span = slice(chunk * CHUNK, (chunk + 1) * CHUNK)
+        lines = chunk * CHUNK + lax.broadcasted_iota(jnp.int32, (SETS, CHUNK), 1)
+        offsets = 1 + (SETS - 1 - lax.broadcasted_iota(jnp.int32, (SETS, CHUNK), 0)) * (
+            (BAND - 2) // (SETS - 1)
+        )
+        blades = []
+        for number in range(kept_first + which, kept_first + which + fix_rows // SETS):
+            starts = offsets + number * BAND
+            inside = (lines >= starts) & (lines < starts + BAND)
+            blades.append(jnp.where(inside, refl[:, span], 0.0))
+        fix_copies[which].wait_recv()
+        high, low = halves(fixes[which])
+        correction = dot3(jnp.concatenate(blades, axis=0).T, high, low)
+        gather_copy(chunk, near_id if which == 0 else far_id).wait_recv()
+        gathered[span] = gathered[span] - correction
+
     def merge(step, carry):
-        pair = lax.rem(step + half // 2, chunks // 2)
+        pair = chunks // 2 - 1 - step
         for which in range(2):
             chunk = 2 * pair + which
-            gather_copy(chunk, near_id if which == 0 else far_id).wait_recv()
+
+            @pl.when(step > 0)
+            def _():
+                gather_copy(chunk, near_id if which == 0 else far_id).wait_recv()
+
             span = pl.ds(pl.multiple_of(chunk * CHUNK, CHUNK), CHUNK)
-            mine = ext[pl.ds(pl.multiple_of(ABOVE + chunk * CHUNK, CHUNK), CHUNK)]
+            mine = ext[span]
             left = jnp.concatenate([mine, gathered[span]], axis=1)
             away = slice(width, 2 * width)
             partial[span] = dot3(left, plan_high[which, :, away], plan_low[which, :, away])
@@ -404,7 +409,7 @@
     lax.fori_loop(0, chunks // 2, merge, 0)
 
     def collect(step, carry):
-        pair = lax.rem(step + half // 2, chunks // 2)
+        pair = chunks // 2 - 1 - step
         for which in range(2):
             chunk = 2 * pair + which
             reduce_copy(chunk, far_id if which == 0 else near_id).wait_recv()
@@ -417,7 +422,7 @@
     for chunk in range(chunks):
         gather_copy(chunk, near_id if chunk % 2 == 0 else far_id).wait_send()
         reduce_copy(chunk, far_id if chunk % 2 == 0 else near_id).wait_send()
-    for copy in table_copies + weight_copies:
+    for copy in table_copies + weight_copies + fix_copies:
         copy.wait_send()
 
     @pl.when(has_prev)
@@ -427,14 +432,15 @@
 
     @pl.when(has_next)
     def _():
-        for copy in to_next:
-            copy.wait_send()
+        to_next.wait_send()
 
 
 def per_device(slab, ranks, poles, roots, flags, reflectors, reflector_scales):
     rows, width = slab.shape
     chunks = rows // CHUNK
-    total = ABOVE + rows + BELOW
+    total = rows + BELOW
+    kept = (RAW * (CHUNK // BAND) + 1) * SETS
+    fix_rows = (RAW // 2 * (CHUNK // BAND) + 2) * SETS
     anywhere = pl.BlockSpec(memory_space=pl.ANY)
     dma = pltpu.SemaphoreType.DMA
     operands = (slab, ranks, poles, roots, flags, reflectors, reflector_scales)
@@ -448,7 +454,6 @@
             pltpu.VMEM((total, width), F32),
             pltpu.VMEM((SETS, total), F32),
             pltpu.VMEM(reflector_scales.shape, F32),
-            pltpu.VMEM(reflector_scales.shape, F32),
             pltpu.VMEM((total, 128), F32),
             pltpu.VMEM((rows, width), F32),
             pltpu.VMEM((4, 8, width), F32),
@@ -459,13 +464,17 @@
             pltpu.VMEM((4 * width, 128), F32),
             pltpu.VMEM((4, 8, width), F32),
             pltpu.VMEM((4 * width, 128), F32),
+            pltpu.VMEM((kept, width), F32),
+            pltpu.VMEM((SETS, width), F32),
+            pltpu.VMEM((2, fix_rows, width), F32),
             pltpu.VMEM((2, 2, 2 * width, width), F32),
             pltpu.VMEM((3, 4 * width, width), F32),
             pltpu.VMEM((2, 2 * width, 2 * width), BF16),
             pltpu.VMEM((2, 2 * width, 2 * width), BF16),
             pltpu.VMEM((rows, width), F32),
             pltpu.VMEM((rows, width), F32),
-            dma((7,)), dma((5,)), dma((5,)), dma((3,)), dma((3,)), dma((3,)), dma((3,)),
+            dma((7,)), dma((3,)), dma((3,)), dma((3,)), dma((3,)), dma((2,)), dma((2,)),
+            dma((3,)), dma((3,)),
             dma((chunks,)), dma((chunks,)), dma((chunks,)), dma((chunks,)),
         ],
         compiler_params=pltpu.CompilerParams(

time: 56.7 us -> 55.6 us (0.981)
  the two profiles are of different devices: /device:TPU:1 before, /device:TPU:0 now
where the time goes in v2:
time: 55.6 us; the launch traced here: 55.4 us
  Pallas kernels  54.1 us (97%)
  local copies, waits for them, and re-layouts  1.32 us (2%)
    pallas_call x1, Pallas kernels, per_device(): pl.pallas_call(kernel, out_shape=pltpu.VMEM((rows, width), F32), in_specs...  54.1 us
    unnamed x1, local copies, waits for them, and re-layouts  1.32 us

profile of v2, /device:TPU:0, one launch (start us, length us, event | category | flops | bytes accessed | tf_op | source)
XLA Modules:
  0.0 55.4 jit_solution(3615309586305130932)
XLA Ops:
  0.0 54.1 %shard_map.73 = f32[2048,256]{1,0:T(8,128)S(1)} custom-call(f32[2048,256]{1,0:T(8,128)} %slab.1, s32[2,256]{1,0:T(2,128)} %ranks.1, f32[2,256]{1,0:T(2,128)} %poles.1, f32[2,256]{1,0:T(2,128)} %roots.1, s32[2,256]{1,0:T(2,128)} %flags.1, f32[8,2048]{1,0:T(8,128)} %reflectors.1, f32[8,16]{1,0:T(8,128)} %scales.1), custom_call_target="tpu_custom_call" | custom-call | tf_op jit(solution)/shard_map/pallas_call | solution.py:448
  54.1 1.3 %copy.9 = f32[2048,256]{1,0:T(8,128)} copy(f32[2048,256]{1,0:T(8,128)S(1)} %shard_map.73) | data formatting | bytes 4194304

commit v3 on v2

--- a/solution.py
+++ b/solution.py
@@ -11,6 +11,7 @@
 SETS = 8
 BELOW = 128
 CHUNK = 256
+PIECE = 128
 RAW = 2
 MESH = pl.DeviceIdType.MESH
 F32 = jnp.float32
@@ -42,7 +43,7 @@
     raw_ints, raw_floats, picked, shared, spread_weights, projections, above, fixes,
     mix_one, mix_two, plan_high, plan_low, partial, arrived,
     local_sems, halo_send, halo_recv, table_send, table_recv, fix_send, fix_recv,
-    weight_send, weight_recv, gather_send, gather_recv, reduce_send, reduce_recv,
+    weight_send, weight_recv, gather_send, gather_recv, reduce_send, reduce_recv, ready,
 ):
     rows = slab.shape[0]
     width = slab.shape[1]
@@ -59,10 +60,24 @@
     near_id = (row, quad + near)
     far_id = (row, quad + far)
     across_id = (row, quad + across)
+    odd = lax.rem(row, 2) == 1
+    even = jnp.logical_not(odd)
     has_prev = row > 0
     has_next = row < row_size - 1
     prev_id = (lax.max(row - 1, 0), col)
     next_id = (lax.min(row + 1, row_size - 1), col)
+
+    barrier = pltpu.get_barrier_semaphore()
+    for partner in (near_id, far_id, across_id):
+        pl.semaphore_signal(barrier, inc=1, device_id=partner, device_id_type=MESH)
+
+    @pl.when(odd & has_prev)
+    def _():
+        pl.semaphore_signal(barrier, inc=1, device_id=prev_id, device_id_type=MESH)
+
+    @pl.when(odd & has_next)
+    def _():
+        pl.semaphore_signal(barrier, inc=1, device_id=next_id, device_id_type=MESH)
 
     own_rows = pl.ds(0, rows)
     own_slab = pltpu.make_async_copy(slab, ext.at[own_rows], local_sems.at[0])
@@ -80,18 +95,6 @@
     own_scale_copy.start()
     own_slab.start()
 
-    barrier = pltpu.get_barrier_semaphore()
-    for partner in (near_id, far_id, across_id):
-        pl.semaphore_signal(barrier, inc=1, device_id=partner, device_id_type=MESH)
-
-    @pl.when(has_prev)
-    def _():
-        pl.semaphore_signal(barrier, inc=1, device_id=prev_id, device_id_type=MESH)
-
-    @pl.when(has_next)
-    def _():
-        pl.semaphore_signal(barrier, inc=1, device_id=next_id, device_id_type=MESH)
-
     for copy in small:
         copy.wait()
     tables[quarter] = jnp.concatenate(
@@ -99,7 +102,7 @@
     )
 
     pl.semaphore_wait(
-        barrier, 3 + jnp.where(has_prev, 1, 0) + jnp.where(has_next, 1, 0)
+        barrier, 3 + jnp.where(even & has_prev, 1, 0) + jnp.where(even & has_next, 1, 0)
     )
 
     def remote(source, target, send, recv, device):
@@ -127,12 +130,15 @@
     for copy in table_copies:
         copy.start()
 
-    def gather_copy(chunk, device):
+    pieces = CHUNK // PIECE
+
+    def gather_copy(chunk, part, device):
         held = slab if isinstance(chunk, int) and chunk >= chunks - RAW else ext
+        span = pl.ds(chunk * CHUNK + part * PIECE, PIECE)
+        number = chunk * pieces + part
         return remote(
-            held.at[pl.ds(chunk * CHUNK, CHUNK)],
-            gathered.at[pl.ds(chunk * CHUNK, CHUNK)],
-            gather_send.at[chunk], gather_recv.at[chunk], device,
+            held.at[span], gathered.at[span],
+            gather_send.at[number], gather_recv.at[number], device,
         )
 
     def reduce_copy(chunk, device):
@@ -142,16 +148,22 @@
             reduce_send.at[chunk], reduce_recv.at[chunk], device,
         )
 
-    def send_chunk(chunk):
-        gather_copy(chunk, near_id if chunk % 2 == 0 else far_id).start()
-
-    for chunk in range(chunks - RAW, chunks):
-        send_chunk(chunk)
-
-    @pl.when(has_prev)
-    def _():
+    def send_pair(pair, parts):
+        for i in parts:
+            gather_copy(2 * pair, i, near_id).start()
+            gather_copy(2 * pair + 1, i, far_id).start()
+
+    send_pair(chunks // 2 - 1, range(pieces))
+
+    @pl.when(even & has_prev)
+    def _():
+        pl.semaphore_signal(ready.at[1], inc=1, device_id=prev_id, device_id_type=MESH)
         for copy in to_prev:
             copy.start()
+
+    @pl.when(even & has_next)
+    def _():
+        pl.semaphore_signal(ready.at[0], inc=1, device_id=next_id, device_id_type=MESH)
 
     @pl.when(jnp.logical_not(has_prev))
     def _():
@@ -193,6 +205,13 @@
     for index in range(SETS):
         for number in range(index, windows - 1):
             sweep(index, number)
+    send_pair(chunks // 2 - 2, range(pieces // 2))
+
+    @pl.when(odd & has_prev)
+    def _():
+        pl.semaphore_wait(ready.at[0], 1)
+        for copy in to_prev:
+            copy.start()
 
     for copy in table_copies:
         copy.wait_recv()
@@ -253,19 +272,6 @@
         alive = tables[quarter, 6 + index : 7 + index] == 0.0
         return jnp.where(alive, jnp.exp(0.5 * total), 0.0)
 
-    @pl.when(has_next)
-    def _():
-        for copy in to_prev:
-            copy.wait_recv()
-
-    turn(windows)
-    for index in range(SETS):
-        sweep(index, windows - 1)
-
-    @pl.when(has_next)
-    def _():
-        to_next.start()
-
     weight_one = weigh(0, half_start, 2 * width, lax.rem(quarter, 2) * width)
     weight_two = weigh(1, 0, 4 * width, quarter * width)
     shared[quarter] = jnp.concatenate([weight_one, weight_two, jnp.zeros((6, width), F32)], axis=0)
@@ -275,8 +281,7 @@
     ]
     for copy in weight_copies:
         copy.start()
-    for chunk in range(chunks - 2 * RAW, chunks - RAW):
-        send_chunk(chunk)
+    send_pair(chunks // 2 - 2, range(pieces // 2, pieces))
 
     def level(index, start, size, store, blocks):
         depth = 128
@@ -315,9 +320,27 @@
 
             lax.fori_loop(0, size // depth, finish, 0, unroll=2)
 
-    fix_rows = (RAW // 2 * per_chunk + 2) * SETS
+    @pl.when(has_next)
+    def _():
+        for copy in to_prev:
+            copy.wait_recv()
+
+    turn(windows)
+    for index in range(SETS):
+        sweep(index, windows - 1)
+
+    @pl.when(odd & has_next)
+    def _():
+        pl.semaphore_wait(ready.at[1], 1)
+
+    @pl.when(has_next)
+    def _():
+        to_next.start()
+
+    fix_rows = (per_chunk + 1) * SETS
     fix_copies = [
-        remote(projections.at[pl.ds(i * SETS, fix_rows)], fixes.at[i],
+        remote(projections.at[pl.ds(i * per_chunk * SETS, fix_rows)],
+               fixes.at[i, pl.ds(0, fix_rows)],
                fix_send.at[i], fix_recv.at[i], device)
         for i, device in enumerate((near_id, far_id))
     ]
@@ -335,8 +358,7 @@
         for number in range(index):
             sweep(index, number)
     for pair in reversed(range(chunks // 2 - RAW)):
-        send_chunk(2 * pair)
-        send_chunk(2 * pair + 1)
+        send_pair(pair, range(pieces))
 
     for copy in weight_copies:
         copy.wait_recv()
@@ -377,14 +399,18 @@
             (BAND - 2) // (SETS - 1)
         )
         blades = []
-        for number in range(kept_first + which, kept_first + which + fix_rows // SETS):
-            starts = offsets + number * BAND
+        for number in range(per_chunk + 1):
+            starts = offsets + (kept_first + which * per_chunk + number) * BAND
             inside = (lines >= starts) & (lines < starts + BAND)
             blades.append(jnp.where(inside, refl[:, span], 0.0))
+        spare = fixes.shape[1] - fix_rows
+        blades.append(jnp.zeros((spare, CHUNK), F32))
         fix_copies[which].wait_recv()
-        high, low = halves(fixes[which])
+        reached = jnp.concatenate([fixes[which, :fix_rows], jnp.zeros((spare, width), F32)], axis=0)
+        high, low = halves(reached)
         correction = dot3(jnp.concatenate(blades, axis=0).T, high, low)
-        gather_copy(chunk, near_id if which == 0 else far_id).wait_recv()
+        for i in range(pieces):
+            gather_copy(chunk, i, near_id if which == 0 else far_id).wait_recv()
         gathered[span] = gathered[span] - correction
 
     def merge(step, carry):
@@ -394,7 +420,8 @@
 
             @pl.when(step > 0)
             def _():
-                gather_copy(chunk, near_id if which == 0 else far_id).wait_recv()
+                for i in range(pieces):
+                    gather_copy(chunk, i, near_id if which == 0 else far_id).wait_recv()
 
             span = pl.ds(pl.multiple_of(chunk * CHUNK, CHUNK), CHUNK)
             mine = ext[span]
@@ -408,31 +435,33 @@
 
     lax.fori_loop(0, chunks // 2, merge, 0)
 
+    for chunk in range(chunks):
+        for i in range(pieces):
+            gather_copy(chunk, i, near_id if chunk % 2 == 0 else far_id).wait_send()
+    for copy in table_copies + weight_copies + fix_copies:
+        copy.wait_send()
+
+    @pl.when(has_prev)
+    def _():
+        for copy in to_prev:
+            copy.wait_send()
+
+    @pl.when(has_next)
+    def _():
+        to_next.wait_send()
+
     def collect(step, carry):
         pair = chunks // 2 - 1 - step
         for which in range(2):
             chunk = 2 * pair + which
-            reduce_copy(chunk, far_id if which == 0 else near_id).wait_recv()
+            copy = reduce_copy(chunk, far_id if which == 0 else near_id)
+            copy.wait_recv()
             span = pl.ds(pl.multiple_of(chunk * CHUNK, CHUNK), CHUNK)
             out[span] = out[span] + arrived[span]
+            copy.wait_send()
         return carry
 
     lax.fori_loop(0, chunks // 2, collect, 0)
-
-    for chunk in range(chunks):
-        gather_copy(chunk, near_id if chunk % 2 == 0 else far_id).wait_send()
-        reduce_copy(chunk, far_id if chunk % 2 == 0 else near_id).wait_send()
-    for copy in table_copies + weight_copies + fix_copies:
-        copy.wait_send()
-
-    @pl.when(has_prev)
-    def _():
-        for copy in to_prev:
-            copy.wait_send()
-
-    @pl.when(has_next)
-    def _():
-        to_next.wait_send()
 
 
 def per_device(slab, ranks, poles, roots, flags, reflectors, reflector_scales):
@@ -440,7 +469,7 @@
     chunks = rows // CHUNK
     total = rows + BELOW
     kept = (RAW * (CHUNK // BAND) + 1) * SETS
-    fix_rows = (RAW // 2 * (CHUNK // BAND) + 2) * SETS
+    fix_rows = (CHUNK // BAND + 2) * SETS
     anywhere = pl.BlockSpec(memory_space=pl.ANY)
     dma = pltpu.SemaphoreType.DMA
     operands = (slab, ranks, poles, roots, flags, reflectors, reflector_scales)
@@ -475,7 +504,8 @@
             pltpu.VMEM((rows, width), F32),
             dma((7,)), dma((3,)), dma((3,)), dma((3,)), dma((3,)), dma((2,)), dma((2,)),
             dma((3,)), dma((3,)),
-            dma((chunks,)), dma((chunks,)), dma((chunks,)), dma((chunks,)),
+            dma((rows // PIECE,)), dma((rows // PIECE,)), dma((chunks,)), dma((chunks,)),
+            pltpu.SemaphoreType.REGULAR((2,)),
         ],
         compiler_params=pltpu.CompilerParams(
             collective_id=0, has_side_effects=True, vmem_limit_bytes=48 * 1024 * 1024

time: 55.6 us -> 53.4 us (0.960)
  Pallas kernels: 54.1 us -> 51.9 us
    pallas_call x1, Pallas kernels: 54.1 us -> 51.9 us  [per_device(): pl.pallas_call(kernel, out_shape=pltpu.VMEM((rows, width), F32), in_specs...]
where the time goes in v3:
time: 53.4 us; the launch traced here: 53.3 us
  Pallas kernels  51.9 us (97%)
  local copies, waits for them, and re-layouts  1.32 us (2%)
    pallas_call x1, Pallas kernels, per_device(): pl.pallas_call(kernel, out_shape=pltpu.VMEM((rows, width), F32), in_specs...  51.9 us
    unnamed x1, local copies, waits for them, and re-layouts  1.32 us

profile of v3, /device:TPU:0, one launch (start us, length us, event | category | flops | bytes accessed | tf_op | source)
XLA Modules:
  0.0 53.3 jit_solution(343819967079733714)
XLA Ops:
  0.0 51.9 %shard_map.73 = f32[2048,256]{1,0:T(8,128)S(1)} custom-call(f32[2048,256]{1,0:T(8,128)} %slab.1, s32[2,256]{1,0:T(2,128)} %ranks.1, f32[2,256]{1,0:T(2,128)} %poles.1, f32[2,256]{1,0:T(2,128)} %roots.1, s32[2,256]{1,0:T(2,128)} %flags.1, f32[8,2048]{1,0:T(8,128)} %reflectors.1, f32[8,16]{1,0:T(8,128)} %scales.1), custom_call_target="tpu_custom_call" | custom-call | tf_op jit(solution)/shard_map/pallas_call | solution.py:477
  51.9 1.3 %copy.9 = f32[2048,256]{1,0:T(8,128)} copy(f32[2048,256]{1,0:T(8,128)S(1)} %shard_map.73) | data formatting | bytes 4194304

commit v4 on v3

--- a/solution.py
+++ b/solution.py
@@ -40,7 +40,7 @@
 def kernel(
     slab, ranks, poles, roots, flags, reflectors, scales, out,
     ext, refl, scales_own, turned, gathered, tables, tall, wide,
-    raw_ints, raw_floats, picked, shared, spread_weights, projections, above, fixes,
+    raw_ints, raw_floats, weight_columns, shared, spread_weights, projections, above, fixes,
     mix_one, mix_two, plan_high, plan_low, partial, arrived,
     local_sems, halo_send, halo_recv, table_send, table_recv, fix_send, fix_recv,
     weight_send, weight_recv, gather_send, gather_recv, reduce_send, reduce_recv, ready,
@@ -216,7 +216,9 @@
     for copy in table_copies:
         copy.wait_recv()
     for i in range(4):
-        wide[:, i * width : (i + 1) * width] = tables[i]
+        span = slice(i * width, (i + 1) * width)
+        wide[:6, span] = tables[i, :6]
+        wide[6:, span] = jnp.where(tables[i, 6:] != 0.0, tables[i, :2], -1.0)
     for i in range(4 * width // BAND):
         tall[i * BAND : (i + 1) * BAND, :SETS] = wide[:, i * BAND : (i + 1) * BAND].T
 
@@ -244,37 +246,45 @@
     )
     half_picked = pick(0, half_ranks, half_start, 2 * width)
     all_picked = pick(1, wide[1:2, :], 0, 4 * width)
-    both = jnp.concatenate(
-        [jnp.concatenate([half_picked, half_picked], axis=1), all_picked]
-        + [jnp.zeros((6, 4 * width), F32)], axis=0
-    )
-    for i in range(4 * width // BAND):
-        picked[i * BAND : (i + 1) * BAND, :SETS] = both[:, i * BAND : (i + 1) * BAND].T
-
-    def weigh(index, start, size, own_start):
+    def weigh(index, pole, root, dead_rank, own_start):
         depth = 64
-        own = tables[quarter, 2 + index : 3 + index]
-        own_place = own_start + lax.broadcasted_iota(jnp.int32, (1, width), 1)
-        positions = lax.broadcasted_iota(jnp.int32, (depth, 1), 0)
-
-        def step(number, total):
-            at = pl.ds(pl.multiple_of(start + number * depth, depth), depth)
+        lanes = lax.broadcasted_iota(jnp.int32, (1, BAND), 1)
+        places = lax.broadcasted_iota(jnp.int32, (depth, 1), 0)
+        living = dead_rank < 0.0
+
+        def step(number, carry):
+            at = pl.ds(pl.multiple_of(quarter * width + number * depth, depth), depth)
+            own = tall[at, 2 + index : 3 + index]
+            own_place = own_start + number * depth + places
+            total = jnp.zeros((depth, BAND), F32)
+            for tile in range(pole.shape[1] // BAND):
+                span = slice(tile * BAND, (tile + 1) * BAND)
+                apart = jnp.abs(pole[:, span] - own)
+                between = jnp.where(lanes + tile * BAND == own_place, 1.0, apart)
+                logs = jnp.log(jnp.abs(root[:, span] - own) / between)
+                total = total + jnp.where(living[:, span], logs, 0.0)
+            alive = tall[at, 6 + index : 7 + index] < 0.0
+            weight = jnp.exp(0.5 * jnp.sum(total, axis=1, keepdims=True))
             within = pl.ds(pl.multiple_of(number * depth, depth), depth)
-            pole = tall[at, 2 + index : 3 + index]
-            living = tall[at, 6 + index : 7 + index] == 0.0
-            root = picked[within, index : index + 1]
-            between = jnp.where(positions + number * depth == own_place, 1.0, jnp.abs(pole - own))
-            logs = jnp.log(jnp.abs(root - own) / between)
-            return total + fold(jnp.where(living, logs, 0.0))
-
-        total = lax.fori_loop(0, size // depth, step, jnp.zeros((8, width), F32), unroll=2)
-        total = jnp.sum(total, axis=0, keepdims=True)
-        alive = tables[quarter, 6 + index : 7 + index] == 0.0
-        return jnp.where(alive, jnp.exp(0.5 * total), 0.0)
-
-    weight_one = weigh(0, half_start, 2 * width, lax.rem(quarter, 2) * width)
-    weight_two = weigh(1, 0, 4 * width, quarter * width)
-    shared[quarter] = jnp.concatenate([weight_one, weight_two, jnp.zeros((6, width), F32)], axis=0)
+            weight_columns[within, index : index + 1] = jnp.where(alive, weight, 0.0)
+            return carry
+
+        lax.fori_loop(0, width // depth, step, 0)
+
+    def half_row(kind):
+        return jnp.concatenate(
+            [wide_part(2 * group)[kind : kind + 1], wide_part(2 * group + 1)[kind : kind + 1]], axis=1
+        )
+
+    def wide_part(number):
+        return wide[:, pl.ds(pl.multiple_of(number * width, width), width)]
+
+    weight_columns[...] = jnp.zeros(weight_columns.shape, F32)
+    weigh(0, half_row(2), half_picked, half_row(6), lax.rem(quarter, 2) * width)
+    weigh(1, wide[3:4, :], all_picked, wide[7:8, :], quarter * width)
+    for i in range(width // BAND):
+        span = slice(i * BAND, (i + 1) * BAND)
+        shared[quarter, :, span] = weight_columns[span, :SETS].T[:2]
     weight_copies = [
         remote(shared.at[quarter], shared.at[quarter], weight_send.at[i], weight_recv.at[i], device)
         for i, device in enumerate((near_id, far_id, across_id))
@@ -284,41 +294,50 @@
     send_pair(chunks // 2 - 2, range(pieces // 2, pieces))
 
     def level(index, start, size, store, blocks):
-        depth = 128
-
-        def column(kind, step):
-            at = pl.ds(pl.multiple_of(start + step * depth, depth), depth)
-            return tall[at, 2 * kind + index : 2 * kind + index + 1]
-
-        for number, (block, within) in enumerate(blocks):
-            root_block = tables[block, 4 + index : 5 + index]
-            here = (within * width + lax.broadcasted_iota(jnp.int32, (1, width), 1)).astype(F32)
-
-            def cauchy(step, carry):
-                norms, dead = carry
-                at = pl.ds(pl.multiple_of(step * depth, depth), depth)
-                shift = pl.ds(pl.multiple_of(start + step * depth, depth), depth)
-                weight = spread_weights[shift, index : index + 1]
-                value = weight / (column(1, step) - root_block)
+        depth = 64
+        roots_of = [tables[block, 4 + index : 5 + index] for block, _ in blocks]
+        ranks_of = [
+            (within * width + lax.broadcasted_iota(jnp.int32, (1, width), 1)).astype(F32)
+            for _, within in blocks
+        ]
+
+        def cauchy(step, carry):
+            at = pl.ds(pl.multiple_of(step * depth, depth), depth)
+            shift = pl.ds(pl.multiple_of(start + step * depth, depth), depth)
+            weight = spread_weights[shift, index : index + 1]
+            pole = tall[shift, 2 + index : 3 + index]
+            dead_rank = tall[shift, 6 + index : 7 + index]
+            sums = []
+            for number in range(len(blocks)):
+                norms, dead = carry[number]
+                value = weight / (pole - roots_of[number])
                 store[number, at] = value
-                norms = norms + jnp.sum(value * value, axis=0, keepdims=True)
-                match = column(0, step) == here
-                dead = dead + jnp.sum(
-                    jnp.where(match, column(3, step), 0.0), axis=0, keepdims=True
+                norms = norms + fold(value * value)
+                dead = dead + fold(jnp.where(dead_rank == ranks_of[number], 1.0, 0.0))
+                sums.append((norms, dead))
+            return tuple(sums)
+
+        zero = jnp.zeros((8, width), F32)
+        sums = lax.fori_loop(0, size // depth, cauchy, ((zero, zero),) * len(blocks))
+        scales_of = [
+            jnp.where(
+                jnp.sum(dead, axis=0, keepdims=True) > 0.0, 0.0,
+                1.0 / jnp.sqrt(jnp.sum(norms, axis=0, keepdims=True)),
+            )
+            for norms, dead in sums
+        ]
+
+        def finish(step, carry):
+            at = pl.ds(pl.multiple_of(step * depth, depth), depth)
+            shift = pl.ds(pl.multiple_of(start + step * depth, depth), depth)
+            dead_rank = tall[shift, 6 + index : 7 + index]
+            for number in range(len(blocks)):
+                store[number, at] = jnp.where(
+                    dead_rank == ranks_of[number], 1.0, store[number, at] * scales_of[number]
                 )
-                return norms, dead
-
-            zero = jnp.zeros((1, width), F32)
-            norms, dead = lax.fori_loop(0, size // depth, cauchy, (zero, zero), unroll=2)
-            inverse = 1.0 / jnp.sqrt(norms)
-
-            def finish(step, carry):
-                at = pl.ds(pl.multiple_of(step * depth, depth), depth)
-                match = (column(0, step) == here).astype(F32)
-                store[number, at] = jnp.where(dead > 0.0, match, store[number, at] * inverse)
-                return carry
-
-            lax.fori_loop(0, size // depth, finish, 0, unroll=2)
+            return carry
+
+        lax.fori_loop(0, size // depth, finish, 0)
 
     @pl.when(has_next)
     def _():
@@ -364,9 +383,9 @@
         copy.wait_recv()
     for i in range(4):
         for j in range(width // BAND):
-            spread_weights[i * width + j * BAND : i * width + (j + 1) * BAND, :SETS] = shared[
-                i, :, j * BAND : (j + 1) * BAND
-            ].T
+            weights = shared[i, :, j * BAND : (j + 1) * BAND]
+            padded = jnp.concatenate([weights, jnp.zeros((6, BAND), F32)], axis=0)
+            spread_weights[i * width + j * BAND : i * width + (j + 1) * BAND, :SETS] = padded.T
     for group in range(2):
         level(
             0, group * 2 * width, 2 * width, mix_one.at[group],
@@ -490,8 +509,8 @@
             pltpu.VMEM((8, 4 * width), F32),
             pltpu.VMEM((2, 2, width), jnp.int32),
             pltpu.VMEM((2, 2, width), F32),
-            pltpu.VMEM((4 * width, 128), F32),
-            pltpu.VMEM((4, 8, width), F32),
+            pltpu.VMEM((width, 128), F32),
+            pltpu.VMEM((4, 2, width), F32),
             pltpu.VMEM((4 * width, 128), F32),
             pltpu.VMEM((kept, width), F32),
             pltpu.VMEM((SETS, width), F32),

time: 53.4 us -> 53.2 us (level)
  no operation moved by 1% of the time
where the time goes in v4:
time: 53.2 us; the launch traced here: 53 us
  Pallas kernels  51.7 us (97%)
  local copies, waits for them, and re-layouts  1.32 us (2%)
    pallas_call x1, Pallas kernels, per_device(): pl.pallas_call(kernel, out_shape=pltpu.VMEM((rows, width), F32), in_specs...  51.7 us
    unnamed x1, local copies, waits for them, and re-layouts  1.32 us

profile of v4, /device:TPU:0, one launch (start us, length us, event | category | flops | bytes accessed | tf_op | source)
XLA Modules:
  0.0 53.0 jit_solution(3347378390197568686)
XLA Ops:
  0.0 51.7 %shard_map.73 = f32[2048,256]{1,0:T(8,128)S(1)} custom-call(f32[2048,256]{1,0:T(8,128)} %slab.1, s32[2,256]{1,0:T(2,128)} %ranks.1, f32[2,256]{1,0:T(2,128)} %poles.1, f32[2,256]{1,0:T(2,128)} %roots.1, s32[2,256]{1,0:T(2,128)} %flags.1, f32[8,2048]{1,0:T(8,128)} %reflectors.1, f32[8,16]{1,0:T(8,128)} %scales.1), custom_call_target="tpu_custom_call" | custom-call | tf_op jit(solution)/shard_map/pallas_call | solution.py:496
  51.7 1.3 %copy.9 = f32[2048,256]{1,0:T(8,128)} copy(f32[2048,256]{1,0:T(8,128)S(1)} %shard_map.73) | data formatting | bytes 4194304

commit v5 on v4

--- a/solution.py
+++ b/solution.py
@@ -12,7 +12,6 @@
 BELOW = 128
 CHUNK = 256
 PIECE = 128
-RAW = 2
 MESH = pl.DeviceIdType.MESH
 F32 = jnp.float32
 BF16 = jnp.bfloat16
@@ -117,8 +116,8 @@
         remote(slab.at[pl.ds(0, BELOW)], ext.at[pl.ds(rows, BELOW)],
                halo_send.at[1], halo_recv.at[1], prev_id),
     ]
-    per_chunk = CHUNK // BAND
-    kept_first = (chunks - RAW) * per_chunk - 1
+    raw_start = (chunks - 1) * CHUNK - PIECE
+    kept_first = raw_start // BAND - 1
     last_window = (windows - 1 - kept_first) * SETS
     to_next = remote(projections.at[pl.ds(last_window, SETS)], above,
                      halo_send.at[2], halo_recv.at[2], next_id)
@@ -132,8 +131,7 @@
 
     pieces = CHUNK // PIECE
 
-    def gather_copy(chunk, part, device):
-        held = slab if isinstance(chunk, int) and chunk >= chunks - RAW else ext
+    def gather_copy(chunk, part, device, held=ext):
         span = pl.ds(chunk * CHUNK + part * PIECE, PIECE)
         number = chunk * pieces + part
         return remote(
@@ -153,7 +151,11 @@
             gather_copy(2 * pair, i, near_id).start()
             gather_copy(2 * pair + 1, i, far_id).start()
 
-    send_pair(chunks // 2 - 1, range(pieces))
+    raw_copies = [
+        gather_copy(chunks - 2, 1, near_id, slab), gather_copy(chunks - 1, 0, far_id, slab)
+    ]
+    for copy in raw_copies:
+        copy.start()
 
     @pl.when(even & has_prev)
     def _():
@@ -202,10 +204,15 @@
         ext[span] = panel - blade * projection
 
     own_slab.wait()
+    early = ((chunks - 3) * CHUNK + PIECE) // BAND
     for index in range(SETS):
-        for number in range(index, windows - 1):
+        for number in range(index, early):
             sweep(index, number)
-    send_pair(chunks // 2 - 2, range(pieces // 2))
+    send_pair(chunks // 2 - 2, range(1))
+    for index in range(SETS):
+        for number in range(early, windows - 1):
+            sweep(index, number)
+    send_pair(chunks // 2 - 2, range(1, pieces))
 
     @pl.when(odd & has_prev)
     def _():
@@ -291,7 +298,15 @@
     ]
     for copy in weight_copies:
         copy.start()
-    send_pair(chunks // 2 - 2, range(pieces // 2, pieces))
+    fix_rows = (PIECE // BAND + 1) * SETS
+    fix_copies = [
+        remote(projections.at[pl.ds(i * SETS, fix_rows)], fixes.at[i],
+               fix_send.at[i], fix_recv.at[i], device)
+        for i, device in enumerate((near_id, far_id))
+    ]
+    for copy in fix_copies:
+        copy.start()
+    gather_copy(chunks - 2, 0, near_id).start()
 
     def level(index, start, size, store, blocks):
         depth = 64
@@ -352,19 +367,11 @@
     def _():
         pl.semaphore_wait(ready.at[1], 1)
 
+    gather_copy(chunks - 1, 1, far_id).start()
+
     @pl.when(has_next)
     def _():
         to_next.start()
-
-    fix_rows = (per_chunk + 1) * SETS
-    fix_copies = [
-        remote(projections.at[pl.ds(i * per_chunk * SETS, fix_rows)],
-               fixes.at[i, pl.ds(0, fix_rows)],
-               fix_send.at[i], fix_recv.at[i], device)
-        for i, device in enumerate((near_id, far_id))
-    ]
-    for copy in fix_copies:
-        copy.start()
 
     @pl.when(has_prev)
     def _():
@@ -376,7 +383,7 @@
         ext[:BAND] = ext[:BAND] - blade * above[index : index + 1]
         for number in range(index):
             sweep(index, number)
-    for pair in reversed(range(chunks // 2 - RAW)):
+    for pair in reversed(range(chunks // 2 - 2)):
         send_pair(pair, range(pieces))
 
     for copy in weight_copies:
@@ -411,36 +418,37 @@
                 plan_high[span] = high
                 plan_low[span] = low
 
-    for which, chunk in enumerate(range(chunks - RAW, chunks)):
-        span = slice(chunk * CHUNK, (chunk + 1) * CHUNK)
-        lines = chunk * CHUNK + lax.broadcasted_iota(jnp.int32, (SETS, CHUNK), 1)
-        offsets = 1 + (SETS - 1 - lax.broadcasted_iota(jnp.int32, (SETS, CHUNK), 0)) * (
+    for which in range(2):
+        start = raw_start + which * PIECE
+        span = slice(start, start + PIECE)
+        lines = start + lax.broadcasted_iota(jnp.int32, (SETS, PIECE), 1)
+        offsets = 1 + (SETS - 1 - lax.broadcasted_iota(jnp.int32, (SETS, PIECE), 0)) * (
             (BAND - 2) // (SETS - 1)
         )
         blades = []
-        for number in range(per_chunk + 1):
-            starts = offsets + (kept_first + which * per_chunk + number) * BAND
+        for number in range(fix_rows // SETS):
+            starts = offsets + (kept_first + which + number) * BAND
             inside = (lines >= starts) & (lines < starts + BAND)
             blades.append(jnp.where(inside, refl[:, span], 0.0))
-        spare = fixes.shape[1] - fix_rows
-        blades.append(jnp.zeros((spare, CHUNK), F32))
         fix_copies[which].wait_recv()
-        reached = jnp.concatenate([fixes[which, :fix_rows], jnp.zeros((spare, width), F32)], axis=0)
-        high, low = halves(reached)
+        high, low = halves(fixes[which])
         correction = dot3(jnp.concatenate(blades, axis=0).T, high, low)
-        for i in range(pieces):
-            gather_copy(chunk, i, near_id if which == 0 else far_id).wait_recv()
+        raw_copies[which].wait_recv()
         gathered[span] = gathered[span] - correction
 
+    def pair_of(step):
+        return jnp.where(step < 2, chunks // 2 - 2 + step, chunks // 2 - 1 - step)
+
     def merge(step, carry):
-        pair = chunks // 2 - 1 - step
+        pair = pair_of(step)
         for which in range(2):
             chunk = 2 * pair + which
 
-            @pl.when(step > 0)
+            gather_copy(chunk, which, near_id if which == 0 else far_id).wait_recv()
+
+            @pl.when(step != 1)
             def _():
-                for i in range(pieces):
-                    gather_copy(chunk, i, near_id if which == 0 else far_id).wait_recv()
+                gather_copy(chunk, 1 - which, near_id if which == 0 else far_id).wait_recv()
 
             span = pl.ds(pl.multiple_of(chunk * CHUNK, CHUNK), CHUNK)
             mine = ext[span]
@@ -470,7 +478,7 @@
         to_next.wait_send()
 
     def collect(step, carry):
-        pair = chunks // 2 - 1 - step
+        pair = pair_of(step)
         for which in range(2):
             chunk = 2 * pair + which
             copy = reduce_copy(chunk, far_id if which == 0 else near_id)
@@ -487,8 +495,8 @@
     rows, width = slab.shape
     chunks = rows // CHUNK
     total = rows + BELOW
-    kept = (RAW * (CHUNK // BAND) + 1) * SETS
-    fix_rows = (CHUNK // BAND + 2) * SETS
+    kept = (CHUNK // BAND + 2) * SETS
+    fix_rows = (PIECE // BAND + 1) * SETS
     anywhere = pl.BlockSpec(memory_space=pl.ANY)
     dma = pltpu.SemaphoreType.DMA
     operands = (slab, ranks, poles, roots, flags, reflectors, reflector_scales)

time: 53.2 us -> 53 us (level)
  no operation moved by 1% of the time
where the time goes in v5:
time: 53 us; the launch traced here: 52.8 us
  Pallas kernels  51.5 us (97%)
  local copies, waits for them, and re-layouts  1.32 us (2%)
    pallas_call x1, Pallas kernels, per_device(): pl.pallas_call(kernel, out_shape=pltpu.VMEM((rows, width), F32), in_specs...  51.5 us
    unnamed x1, local copies, waits for them, and re-layouts  1.32 us

profile of v5, /device:TPU:0, one launch (start us, length us, event | category | flops | bytes accessed | tf_op | source)
XLA Modules:
  0.0 52.8 jit_solution(16281274327839860571)
XLA Ops:
  0.0 51.5 %shard_map.73 = f32[2048,256]{1,0:T(8,128)S(1)} custom-call(f32[2048,256]{1,0:T(8,128)} %slab.1, s32[2,256]{1,0:T(2,128)} %ranks.1, f32[2,256]{1,0:T(2,128)} %poles.1, f32[2,256]{1,0:T(2,128)} %roots.1, s32[2,256]{1,0:T(2,128)} %flags.1, f32[8,2048]{1,0:T(8,128)} %reflectors.1, f32[8,16]{1,0:T(8,128)} %scales.1), custom_call_target="tpu_custom_call" | custom-call | tf_op jit(solution)/shard_map/pallas_call | solution.py:504
  51.5 1.3 %copy.9 = f32[2048,256]{1,0:T(8,128)} copy(f32[2048,256]{1,0:T(8,128)S(1)} %shard_map.73) | data formatting | bytes 4194304

commit v6 on v4

--- a/solution.py
+++ b/solution.py
@@ -12,7 +12,6 @@
 BELOW = 128
 CHUNK = 256
 PIECE = 128
-RAW = 2
 MESH = pl.DeviceIdType.MESH
 F32 = jnp.float32
 BF16 = jnp.bfloat16
@@ -40,10 +39,10 @@
 def kernel(
     slab, ranks, poles, roots, flags, reflectors, scales, out,
     ext, refl, scales_own, turned, gathered, tables, tall, wide,
-    raw_ints, raw_floats, weight_columns, shared, spread_weights, projections, above, fixes,
+    raw_ints, raw_floats, weights, projections, above, fixes,
     mix_one, mix_two, plan_high, plan_low, partial, arrived,
     local_sems, halo_send, halo_recv, table_send, table_recv, fix_send, fix_recv,
-    weight_send, weight_recv, gather_send, gather_recv, reduce_send, reduce_recv, ready,
+    gather_send, gather_recv, reduce_send, reduce_recv, ready,
 ):
     rows = slab.shape[0]
     width = slab.shape[1]
@@ -117,8 +116,8 @@
         remote(slab.at[pl.ds(0, BELOW)], ext.at[pl.ds(rows, BELOW)],
                halo_send.at[1], halo_recv.at[1], prev_id),
     ]
-    per_chunk = CHUNK // BAND
-    kept_first = (chunks - RAW) * per_chunk - 1
+    raw_start = (chunks - 1) * CHUNK - PIECE
+    kept_first = raw_start // BAND - 1
     last_window = (windows - 1 - kept_first) * SETS
     to_next = remote(projections.at[pl.ds(last_window, SETS)], above,
                      halo_send.at[2], halo_recv.at[2], next_id)
@@ -132,8 +131,7 @@
 
     pieces = CHUNK // PIECE
 
-    def gather_copy(chunk, part, device):
-        held = slab if isinstance(chunk, int) and chunk >= chunks - RAW else ext
+    def gather_copy(chunk, part, device, held=ext):
         span = pl.ds(chunk * CHUNK + part * PIECE, PIECE)
         number = chunk * pieces + part
         return remote(
@@ -153,7 +151,11 @@
             gather_copy(2 * pair, i, near_id).start()
             gather_copy(2 * pair + 1, i, far_id).start()
 
-    send_pair(chunks // 2 - 1, range(pieces))
+    raw_copies = [
+        gather_copy(chunks - 2, 1, near_id, slab), gather_copy(chunks - 1, 0, far_id, slab)
+    ]
+    for copy in raw_copies:
+        copy.start()
 
     @pl.when(even & has_prev)
     def _():
@@ -202,16 +204,50 @@
         ext[span] = panel - blade * projection
 
     own_slab.wait()
+    early = ((chunks - 3) * CHUNK + PIECE) // BAND
     for index in range(SETS):
-        for number in range(index, windows - 1):
+        for number in range(index, early):
             sweep(index, number)
-    send_pair(chunks // 2 - 2, range(pieces // 2))
+    send_pair(chunks // 2 - 2, range(1))
+    for index in range(SETS):
+        for number in range(early, windows - 1):
+            sweep(index, number)
+    send_pair(chunks // 2 - 2, range(1, pieces))
 
     @pl.when(odd & has_prev)
     def _():
         pl.semaphore_wait(ready.at[0], 1)
         for copy in to_prev:
             copy.start()
+
+    fix_rows = (PIECE // BAND + 1) * SETS
+    fix_copies = [
+        remote(projections.at[pl.ds(i * SETS, fix_rows)], fixes.at[i],
+               fix_send.at[i], fix_recv.at[i], device)
+        for i, device in enumerate((near_id, far_id))
+    ]
+    for copy in fix_copies:
+        copy.start()
+    gather_copy(chunks - 2, 0, near_id).start()
+
+    @pl.when(has_next)
+    def _():
+        for copy in to_prev:
+            copy.wait_recv()
+
+    turn(windows)
+    for index in range(SETS):
+        sweep(index, windows - 1)
+
+    @pl.when(odd & has_next)
+    def _():
+        pl.semaphore_wait(ready.at[1], 1)
+
+    gather_copy(chunks - 1, 1, far_id).start()
+
+    @pl.when(has_next)
+    def _():
+        to_next.start()
 
     for copy in table_copies:
         copy.wait_recv()
@@ -222,8 +258,6 @@
     for i in range(4 * width // BAND):
         tall[i * BAND : (i + 1) * BAND, :SETS] = wide[:, i * BAND : (i + 1) * BAND].T
 
-    half_start = lax.rem(quarter // 2, 2) * 2 * width
-
     def fold(value):
         return jnp.sum(value.reshape(value.shape[0] // 8, 8, value.shape[1]), axis=0)
 
@@ -237,61 +271,52 @@
             root = tall[at, 4 + index : 5 + index]
             return total + fold(jnp.where(ranks_row == here, root, 0.0))
 
-        total = lax.fori_loop(0, size // depth, step, jnp.zeros((8, size), F32))
+        total = lax.fori_loop(0, size // depth, step, jnp.zeros((8, size), F32), unroll=4)
         return jnp.sum(total, axis=0, keepdims=True)
 
-    group = quarter // 2
-    half_ranks = jnp.concatenate(
-        [tables[2 * group, 0:1], tables[2 * group + 1, 0:1]], axis=1
-    )
-    half_picked = pick(0, half_ranks, half_start, 2 * width)
-    all_picked = pick(1, wide[1:2, :], 0, 4 * width)
-    def weigh(index, pole, root, dead_rank, own_start):
+    def weigh(index, start, size):
         depth = 64
+        span = slice(start, start + size)
+        root = pick(index, wide[index : index + 1, span], start, size)
+        pole = wide[2 + index : 3 + index, span]
+        living = wide[6 + index : 7 + index, span] < 0.0
         lanes = lax.broadcasted_iota(jnp.int32, (1, BAND), 1)
         places = lax.broadcasted_iota(jnp.int32, (depth, 1), 0)
-        living = dead_rank < 0.0
 
         def step(number, carry):
-            at = pl.ds(pl.multiple_of(quarter * width + number * depth, depth), depth)
+            at = pl.ds(pl.multiple_of(start + number * depth, depth), depth)
             own = tall[at, 2 + index : 3 + index]
-            own_place = own_start + number * depth + places
+            own_place = number * depth + places
             total = jnp.zeros((depth, BAND), F32)
-            for tile in range(pole.shape[1] // BAND):
-                span = slice(tile * BAND, (tile + 1) * BAND)
-                apart = jnp.abs(pole[:, span] - own)
+            for tile in range(size // BAND):
+                part = slice(tile * BAND, (tile + 1) * BAND)
+                apart = jnp.abs(pole[:, part] - own)
                 between = jnp.where(lanes + tile * BAND == own_place, 1.0, apart)
-                logs = jnp.log(jnp.abs(root[:, span] - own) / between)
-                total = total + jnp.where(living[:, span], logs, 0.0)
+                logs = jnp.log(jnp.abs(root[:, part] - own) / between)
+                total = total + jnp.where(living[:, part], logs, 0.0)
             alive = tall[at, 6 + index : 7 + index] < 0.0
             weight = jnp.exp(0.5 * jnp.sum(total, axis=1, keepdims=True))
-            within = pl.ds(pl.multiple_of(number * depth, depth), depth)
-            weight_columns[within, index : index + 1] = jnp.where(alive, weight, 0.0)
+            weights[at, index : index + 1] = jnp.where(alive, weight, 0.0)
             return carry
 
-        lax.fori_loop(0, width // depth, step, 0)
-
-    def half_row(kind):
-        return jnp.concatenate(
-            [wide_part(2 * group)[kind : kind + 1], wide_part(2 * group + 1)[kind : kind + 1]], axis=1
-        )
-
-    def wide_part(number):
-        return wide[:, pl.ds(pl.multiple_of(number * width, width), width)]
-
-    weight_columns[...] = jnp.zeros(weight_columns.shape, F32)
-    weigh(0, half_row(2), half_picked, half_row(6), lax.rem(quarter, 2) * width)
-    weigh(1, wide[3:4, :], all_picked, wide[7:8, :], quarter * width)
-    for i in range(width // BAND):
-        span = slice(i * BAND, (i + 1) * BAND)
-        shared[quarter, :, span] = weight_columns[span, :SETS].T[:2]
-    weight_copies = [
-        remote(shared.at[quarter], shared.at[quarter], weight_send.at[i], weight_recv.at[i], device)
-        for i, device in enumerate((near_id, far_id, across_id))
-    ]
-    for copy in weight_copies:
-        copy.start()
-    send_pair(chunks // 2 - 2, range(pieces // 2, pieces))
+        lax.fori_loop(0, size // depth, step, 0, unroll=4)
+
+    weigh(0, 0, 2 * width)
+    weigh(0, 2 * width, 2 * width)
+    weigh(1, 0, 4 * width)
+
+    @pl.when(has_prev)
+    def _():
+        to_next.wait_recv()
+
+    head = lax.broadcasted_iota(jnp.int32, (BAND, 1), 0)
+    for index in range(SETS):
+        blade = jnp.where(head < set_offset(index), turned[:BAND, index : index + 1], 0.0)
+        ext[:BAND] = ext[:BAND] - blade * above[index : index + 1]
+        for number in range(index):
+            sweep(index, number)
+    for pair in reversed(range(chunks // 2 - 2)):
+        send_pair(pair, range(pieces))
 
     def level(index, start, size, store, blocks):
         depth = 64
@@ -304,7 +329,7 @@
         def cauchy(step, carry):
             at = pl.ds(pl.multiple_of(step * depth, depth), depth)
             shift = pl.ds(pl.multiple_of(start + step * depth, depth), depth)
-            weight = spread_weights[shift, index : index + 1]
+            weight = weights[shift, index : index + 1]
             pole = tall[shift, 2 + index : 3 + index]
             dead_rank = tall[shift, 6 + index : 7 + index]
             sums = []
@@ -318,7 +343,7 @@
             return tuple(sums)
 
         zero = jnp.zeros((8, width), F32)
-        sums = lax.fori_loop(0, size // depth, cauchy, ((zero, zero),) * len(blocks))
+        sums = lax.fori_loop(0, size // depth, cauchy, ((zero, zero),) * len(blocks), unroll=4)
         scales_of = [
             jnp.where(
                 jnp.sum(dead, axis=0, keepdims=True) > 0.0, 0.0,
@@ -337,55 +362,8 @@
                 )
             return carry
 
-        lax.fori_loop(0, size // depth, finish, 0)
-
-    @pl.when(has_next)
-    def _():
-        for copy in to_prev:
-            copy.wait_recv()
-
-    turn(windows)
-    for index in range(SETS):
-        sweep(index, windows - 1)
-
-    @pl.when(odd & has_next)
-    def _():
-        pl.semaphore_wait(ready.at[1], 1)
-
-    @pl.when(has_next)
-    def _():
-        to_next.start()
-
-    fix_rows = (per_chunk + 1) * SETS
-    fix_copies = [
-        remote(projections.at[pl.ds(i * per_chunk * SETS, fix_rows)],
-               fixes.at[i, pl.ds(0, fix_rows)],
-               fix_send.at[i], fix_recv.at[i], device)
-        for i, device in enumerate((near_id, far_id))
-    ]
-    for copy in fix_copies:
-        copy.start()
-
-    @pl.when(has_prev)
-    def _():
-        to_next.wait_recv()
-
-    head = lax.broadcasted_iota(jnp.int32, (BAND, 1), 0)
-    for index in range(SETS):
-        blade = jnp.where(head < set_offset(index), turned[:BAND, index : index + 1], 0.0)
-        ext[:BAND] = ext[:BAND] - blade * above[index : index + 1]
-        for number in range(index):
-            sweep(index, number)
-    for pair in reversed(range(chunks // 2 - RAW)):
-        send_pair(pair, range(pieces))
-
-    for copy in weight_copies:
-        copy.wait_recv()
-    for i in range(4):
-        for j in range(width // BAND):
-            weights = shared[i, :, j * BAND : (j + 1) * BAND]
-            padded = jnp.concatenate([weights, jnp.zeros((6, BAND), F32)], axis=0)
-            spread_weights[i * width + j * BAND : i * width + (j + 1) * BAND, :SETS] = padded.T
+        lax.fori_loop(0, size // depth, finish, 0, unroll=4)
+
     for group in range(2):
         level(
             0, group * 2 * width, 2 * width, mix_one.at[group],
@@ -411,36 +389,37 @@
                 plan_high[span] = high
                 plan_low[span] = low
 
-    for which, chunk in enumerate(range(chunks - RAW, chunks)):
-        span = slice(chunk * CHUNK, (chunk + 1) * CHUNK)
-        lines = chunk * CHUNK + lax.broadcasted_iota(jnp.int32, (SETS, CHUNK), 1)
-        offsets = 1 + (SETS - 1 - lax.broadcasted_iota(jnp.int32, (SETS, CHUNK), 0)) * (
+    for which in range(2):
+        start = raw_start + which * PIECE
+        span = slice(start, start + PIECE)
+        lines = start + lax.broadcasted_iota(jnp.int32, (SETS, PIECE), 1)
+        offsets = 1 + (SETS - 1 - lax.broadcasted_iota(jnp.int32, (SETS, PIECE), 0)) * (
             (BAND - 2) // (SETS - 1)
         )
         blades = []
-        for number in range(per_chunk + 1):
-            starts = offsets + (kept_first + which * per_chunk + number) * BAND
+        for number in range(fix_rows // SETS):
+            starts = offsets + (kept_first + which + number) * BAND
             inside = (lines >= starts) & (lines < starts + BAND)
             blades.append(jnp.where(inside, refl[:, span], 0.0))
-        spare = fixes.shape[1] - fix_rows
-        blades.append(jnp.zeros((spare, CHUNK), F32))
         fix_copies[which].wait_recv()
-        reached = jnp.concatenate([fixes[which, :fix_rows], jnp.zeros((spare, width), F32)], axis=0)
-        high, low = halves(reached)
+        high, low = halves(fixes[which])
         correction = dot3(jnp.concatenate(blades, axis=0).T, high, low)
-        for i in range(pieces):
-            gather_copy(chunk, i, near_id if which == 0 else far_id).wait_recv()
+        raw_copies[which].wait_recv()
         gathered[span] = gathered[span] - correction
 
+    def pair_of(step):
+        return jnp.where(step < 2, chunks // 2 - 2 + step, chunks // 2 - 1 - step)
+
     def merge(step, carry):
-        pair = chunks // 2 - 1 - step
+        pair = pair_of(step)
         for which in range(2):
             chunk = 2 * pair + which
 
-            @pl.when(step > 0)
+            gather_copy(chunk, which, near_id if which == 0 else far_id).wait_recv()
+
+            @pl.when(step != 1)
             def _():
-                for i in range(pieces):
-                    gather_copy(chunk, i, near_id if which == 0 else far_id).wait_recv()
+                gather_copy(chunk, 1 - which, near_id if which == 0 else far_id).wait_recv()
 
             span = pl.ds(pl.multiple_of(chunk * CHUNK, CHUNK), CHUNK)
             mine = ext[span]
@@ -457,7 +436,7 @@
     for chunk in range(chunks):
         for i in range(pieces):
             gather_copy(chunk, i, near_id if chunk % 2 == 0 else far_id).wait_send()
-    for copy in table_copies + weight_copies + fix_copies:
+    for copy in table_copies + fix_copies:
         copy.wait_send()
 
     @pl.when(has_prev)
@@ -470,7 +449,7 @@
         to_next.wait_send()
 
     def collect(step, carry):
-        pair = chunks // 2 - 1 - step
+        pair = pair_of(step)
         for which in range(2):
             chunk = 2 * pair + which
             copy = reduce_copy(chunk, far_id if which == 0 else near_id)
@@ -487,8 +466,8 @@
     rows, width = slab.shape
     chunks = rows // CHUNK
     total = rows + BELOW
-    kept = (RAW * (CHUNK // BAND) + 1) * SETS
-    fix_rows = (CHUNK // BAND + 2) * SETS
+    kept = (CHUNK // BAND + 2) * SETS
+    fix_rows = (PIECE // BAND + 1) * SETS
     anywhere = pl.BlockSpec(memory_space=pl.ANY)
     dma = pltpu.SemaphoreType.DMA
     operands = (slab, ranks, poles, roots, flags, reflectors, reflector_scales)
@@ -509,8 +488,6 @@
             pltpu.VMEM((8, 4 * width), F32),
             pltpu.VMEM((2, 2, width), jnp.int32),
             pltpu.VMEM((2, 2, width), F32),
-            pltpu.VMEM((width, 128), F32),
-            pltpu.VMEM((4, 2, width), F32),
             pltpu.VMEM((4 * width, 128), F32),
             pltpu.VMEM((kept, width), F32),
             pltpu.VMEM((SETS, width), F32),
@@ -522,7 +499,6 @@
             pltpu.VMEM((rows, width), F32),
             pltpu.VMEM((rows, width), F32),
             dma((7,)), dma((3,)), dma((3,)), dma((3,)), dma((3,)), dma((2,)), dma((2,)),
-            dma((3,)), dma((3,)),
             dma((rows // PIECE,)), dma((rows // PIECE,)), dma((chunks,)), dma((chunks,)),
             pltpu.SemaphoreType.REGULAR((2,)),
         ],

time: 53.2 us -> 52.3 us (0.983)
  Pallas kernels: 51.7 us -> 50.9 us
    pallas_call x1, Pallas kernels: 51.7 us -> 50.9 us  [per_device(): pl.pallas_call(kernel, out_shape=pltpu.VMEM((rows, width), F32), in_specs...]
where the time goes in v6:
time: 52.3 us; the launch traced here: 52.2 us
  Pallas kernels  50.9 us (97%)
  local copies, waits for them, and re-layouts  1.32 us (3%)
    pallas_call x1, Pallas kernels, per_device(): pl.pallas_call(kernel, out_shape=pltpu.VMEM((rows, width), F32), in_specs...  50.9 us
    unnamed x1, local copies, waits for them, and re-layouts  1.32 us

profile of v6, /device:TPU:0, one launch (start us, length us, event | category | flops | bytes accessed | tf_op | source)
XLA Modules:
  0.0 52.2 jit_solution(9570876239654408788)
XLA Ops:
  0.0 50.9 %shard_map.73 = f32[2048,256]{1,0:T(8,128)S(1)} custom-call(f32[2048,256]{1,0:T(8,128)} %slab.1, s32[2,256]{1,0:T(2,128)} %ranks.1, f32[2,256]{1,0:T(2,128)} %poles.1, f32[2,256]{1,0:T(2,128)} %roots.1, s32[2,256]{1,0:T(2,128)} %flags.1, f32[8,2048]{1,0:T(8,128)} %reflectors.1, f32[8,16]{1,0:T(8,128)} %scales.1), custom_call_target="tpu_custom_call" | custom-call | tf_op jit(solution)/shard_map/pallas_call | solution.py:475
  50.9 1.3 %copy.9 = f32[2048,256]{1,0:T(8,128)} copy(f32[2048,256]{1,0:T(8,128)S(1)} %shard_map.73) | data formatting | bytes 4194304

commit v7 on v6

--- a/solution.py
+++ b/solution.py
@@ -301,22 +301,25 @@
 
         lax.fori_loop(0, size // depth, step, 0, unroll=4)
 
+    def head_sweeps():
+        @pl.when(has_prev)
+        def _():
+            to_next.wait_recv()
+
+        head = lax.broadcasted_iota(jnp.int32, (BAND, 1), 0)
+        for index in range(SETS):
+            blade = jnp.where(head < set_offset(index), turned[:BAND, index : index + 1], 0.0)
+            ext[:BAND] = ext[:BAND] - blade * above[index : index + 1]
+            for number in range(index):
+                sweep(index, number)
+        for pair in reversed(range(chunks // 2 - 2)):
+            send_pair(pair, range(pieces))
+
+    weigh(1, 0, 4 * width)
+    pl.when(even)(head_sweeps)
     weigh(0, 0, 2 * width)
     weigh(0, 2 * width, 2 * width)
-    weigh(1, 0, 4 * width)
-
-    @pl.when(has_prev)
-    def _():
-        to_next.wait_recv()
-
-    head = lax.broadcasted_iota(jnp.int32, (BAND, 1), 0)
-    for index in range(SETS):
-        blade = jnp.where(head < set_offset(index), turned[:BAND, index : index + 1], 0.0)
-        ext[:BAND] = ext[:BAND] - blade * above[index : index + 1]
-        for number in range(index):
-            sweep(index, number)
-    for pair in reversed(range(chunks // 2 - 2)):
-        send_pair(pair, range(pieces))
+    pl.when(odd)(head_sweeps)
 
     def level(index, start, size, store, blocks):
         depth = 64

time: 52.3 us -> 52.3 us (level)
  no operation moved by 1% of the time
where the time goes in v7:
time: 52.3 us; the launch traced here: 52.2 us
  Pallas kernels  50.9 us (97%)
  local copies, waits for them, and re-layouts  1.32 us (3%)
    pallas_call x1, Pallas kernels, per_device(): pl.pallas_call(kernel, out_shape=pltpu.VMEM((rows, width), F32), in_specs...  50.9 us
    unnamed x1, local copies, waits for them, and re-layouts  1.32 us

profile of v7, /device:TPU:0, one launch (start us, length us, event | category | flops | bytes accessed | tf_op | source)
XLA Modules:
  0.0 52.2 jit_solution(14292746642905507992)
XLA Ops:
  0.0 50.9 %shard_map.73 = f32[2048,256]{1,0:T(8,128)S(1)} custom-call(f32[2048,256]{1,0:T(8,128)} %slab.1, s32[2,256]{1,0:T(2,128)} %ranks.1, f32[2,256]{1,0:T(2,128)} %poles.1, f32[2,256]{1,0:T(2,128)} %roots.1, s32[2,256]{1,0:T(2,128)} %flags.1, f32[8,2048]{1,0:T(8,128)} %reflectors.1, f32[8,16]{1,0:T(8,128)} %scales.1), custom_call_target="tpu_custom_call" | custom-call | tf_op jit(solution)/shard_map/pallas_call | solution.py:478
  50.9 1.3 %copy.9 = f32[2048,256]{1,0:T(8,128)} copy(f32[2048,256]{1,0:T(8,128)S(1)} %shard_map.73) | data formatting | bytes 4194304
